TPU v7x, 128 devices: a whole 4x4x4 slice. The times are simulated.
128 devices in a mesh: fsdp: 8 (over z_hi, x), ctx: 16 (over z_lo, y, core).
Axes of the slice: x: 4, y: 4, z: 4 (z_hi: 2, z_lo: 2; z = z_hi * 2 + z_lo), core: 2. Of those that a mesh axis runs over, the one named last changes fastest.
Arguments:
- tokens: bfloat16 [8, 4096, 576], P('fsdp', 'ctx'), may hold values from -6 to 6
- positions: int32 [8, 4096], P('fsdp', 'ctx'), may hold values from 0 to 4095, as said below
- norm1_gain: bfloat16 [576], P('fsdp'), may hold values from 0.5 to 1.5
- w_query: bfloat16 [576, 576], P('fsdp'), may hold values from -0.25 to 0.25
- keyvalue_projection: bfloat16 [576, 384], P('fsdp'), may hold values from -0.25 to 0.25
- w_out: bfloat16 [576, 576], P(None, 'fsdp'), may hold values from -6 to 6
- norm2_gain: bfloat16 [576], P('fsdp'), may hold values from 0.5 to 1.5
- w_gate: bfloat16 [576, 1536], P('fsdp'), may hold values from -0.25 to 0.25
- w_up: bfloat16 [576, 1536], P('fsdp'), may hold values from -0.25 to 0.25
- w_down: bfloat16 [1536, 576], P(None, 'fsdp'), may hold values from -0.15625 to 0.15625
- cotangent: bfloat16 [8, 4096, 576], P('fsdp', 'ctx'), may hold values from -6 to 6
Outputs:
- block_out: bfloat16 [8, 4096, 576], P('fsdp', 'ctx')
- input_grad: float32 [8, 4096, 576], P('fsdp', 'ctx')
- grad_norm1: float32 [576], P('fsdp')
- grad_query: float32 [576, 576], P('fsdp')
- grad_keyvalue: float32 [576, 384], P('fsdp')
- grad_out: float32 [576, 576], P(None, 'fsdp')
- grad_norm2: float32 [576], P('fsdp')
- grad_gate: float32 [576, 1536], P('fsdp')
- grad_up: float32 [576, 1536], P('fsdp')
- grad_down: float32 [1536, 576], P(None, 'fsdp')
Inputs may be any that keep to these rules, and one draw needn't show every extreme that they name: Each sequence's positions are a permutation of 0 to 4095 made of aligned runs of 128 stored tokens holding consecutive positions in increasing order.
All inputs are finite; a program needn't handle non-finite values.
Results may differ from a plain program's by a relative error of at most 0.025.
Values may be sent and summed in bfloat16 or wider, within the bound.
A program may use at most 128 MiB of HBM per device.

v0:
```python
import math

import jax
import jax.numpy as jnp
from jax import lax
from jax.sharding import PartitionSpec as P

HEAD_SIZE = 64


def angles(pos, width):
    half = width // 2
    freqs = jnp.power(
        jnp.float32(100000.0), -(jnp.arange(half).astype(jnp.float32) * (2.0 / width))
    )
    angle = pos.astype(jnp.float32)[:, None] * freqs[None, :]
    return (jnp.cos(angle)[:, None, :], jnp.sin(angle)[:, None, :])


def rotate_pairs(value_rows, cosine_table, sine_table):
    half = value_rows.shape[-1] // 2
    first = value_rows[..., :half]
    second = value_rows[..., half:]
    return jnp.concatenate(
        [first * cosine_table - second * sine_table, second * cosine_table + first * sine_table],
        axis=-1,
    )


def unrotate(value_rows, cosine_table, sine_table):
    half = value_rows.shape[-1] // 2
    first = value_rows[..., :half]
    second = value_rows[..., half:]
    return jnp.concatenate(
        [first * cosine_table + second * sine_table, second * cosine_table - first * sine_table],
        axis=-1,
    )


def normalize(value_rows, gain):
    factor = lax.rsqrt(jnp.mean(value_rows * value_rows, axis=-1, keepdims=True) + 1e-05)
    return (value_rows * factor * gain, factor)


def norm_back(value_rows, factor, gain, upstream):
    weighted = upstream * gain
    inner = jnp.mean(weighted * value_rows, axis=-1, keepdims=True)
    grad_in = factor * weighted - value_rows * (factor * factor * factor) * inner
    return (grad_in, jnp.sum(upstream * value_rows * factor, axis=0))


def forward_fold(queries, query_pos, scale):
    rows, groups, share, width = queries.shape

    def fold(carry, piece, start):
        block_kv, block_pos = piece
        count = block_kv.shape[0] // rows
        kv_blocks = block_kv.reshape(count, rows, 2, groups, width)
        pos_blocks = block_pos.reshape(count, rows)

        def inner(state, item):
            running_max, running_total, running_acc = state
            kv_block, key_pos = item
            scores = (
                jnp.einsum(
                    "tgrd,kgd->tgrk", queries, kv_block[:, 0], preferred_element_type=jnp.float32
                )
                * scale
            )
            allowed = key_pos[None, None, None, :] <= query_pos[:, None, None, None]
            scores = jnp.where(allowed, scores, -1e30)
            new_max = jnp.maximum(running_max, jnp.max(scores, axis=-1))
            probs = jnp.where(allowed, jnp.exp(scores - new_max[..., None]), 0.0)
            factor = jnp.exp(running_max - new_max)
            running_total = running_total * factor + jnp.sum(probs, axis=-1)
            update = jnp.einsum(
                "tgrk,kgd->tgrd",
                probs.astype(jnp.bfloat16),
                kv_block[:, 1],
                preferred_element_type=jnp.float32,
            )
            running_acc = running_acc * factor[..., None] + update
            return ((new_max, running_total, running_acc), None)

        carry, unused = lax.scan(inner, carry, (kv_blocks, pos_blocks))
        return carry

    return fold


def backward_fold(queries, query_pos, log_total, grad_att, delta, scale):
    rows, groups, share, width = queries.shape

    def fold(carry, piece, start):
        block_kv, block_pos = piece
        count = block_kv.shape[0] // rows
        kv_blocks = block_kv.reshape(count, rows, 2, groups, width)
        pos_blocks = block_pos.reshape(count, rows)

        def inner(state, item):
            kv_block, key_pos, index = item
            key_rows = kv_block[:, 0]
            value_rows = kv_block[:, 1]
            scores = (
                jnp.einsum("tgrd,kgd->tgrk", queries, key_rows, preferred_element_type=jnp.float32)
                * scale
            )
            allowed = key_pos[None, None, None, :] <= query_pos[:, None, None, None]
            probs = jnp.where(allowed, jnp.exp(scores - log_total[..., None]), 0.0)
            grad_prob = jnp.einsum(
                "tgrd,kgd->tgrk", grad_att, value_rows, preferred_element_type=jnp.float32
            )
            grad_score = (probs * (grad_prob - delta[..., None])).astype(jnp.bfloat16)
            grad_query = (
                state[0]
                + jnp.einsum(
                    "tgrk,kgd->tgrd", grad_score, key_rows, preferred_element_type=jnp.float32
                )
                * scale
            )
            grad_kv = state[1]
            grad_keys = (
                jnp.einsum(
                    "tgrk,tgrd->kgd", grad_score, queries, preferred_element_type=jnp.float32
                )
                * scale
            )
            grad_values = jnp.einsum(
                "tgrk,tgrd->kgd",
                probs.astype(jnp.bfloat16),
                grad_att,
                preferred_element_type=jnp.float32,
            )
            begin = index * rows
            previous = lax.dynamic_slice_in_dim(grad_kv, begin, rows, 0)
            grad_kv = lax.dynamic_update_slice_in_dim(
                grad_kv, previous + jnp.stack([grad_keys, grad_values], axis=1), begin, 0
            )
            return ((grad_query, grad_kv), None)

        carry, unused = lax.scan(
            inner, carry, (kv_blocks, pos_blocks, jnp.arange(count, dtype=jnp.int32))
        )
        return carry

    return fold


def local(
    tokens,
    positions,
    norm1_gain,
    w_query,
    keyvalue_projection,
    w_out,
    norm2_gain,
    w_gate,
    w_up,
    w_down,
    cotangent,
):
    inputs = tokens[0].astype(jnp.float32)
    token_pos = positions[0]
    rows = inputs.shape[0]
    heads_kv = keyvalue_projection.shape[1] // (2 * HEAD_SIZE)
    share = w_query.shape[1] // (HEAD_SIZE * heads_kv)
    sequence_length = rows * lax.axis_size("ctx")
    scale = 1.0 / math.sqrt(HEAD_SIZE)
    cosine_table, sine_table = angles(token_pos, HEAD_SIZE)
    gain_one, query_full, keyvalue_full, out_full = (
        lax.all_gather(norm1_gain, "fsdp", axis=0, tiled=True),
        lax.all_gather(w_query, "fsdp", axis=0, tiled=True),
        lax.all_gather(keyvalue_projection, "fsdp", axis=0, tiled=True),
        lax.all_gather(w_out, "fsdp", axis=1, tiled=True),
    )
    normed_one, factor_one = normalize(inputs, gain_one.astype(jnp.float32))
    first_activation = normed_one.astype(jnp.bfloat16)
    query_pre = jnp.dot(first_activation, query_full, preferred_element_type=jnp.float32).reshape(
        rows, heads_kv * share, HEAD_SIZE
    )
    keyvalue_before_rotation = jnp.dot(
        first_activation, keyvalue_full, preferred_element_type=jnp.float32
    ).reshape(rows, 2 * heads_kv, HEAD_SIZE)
    queries = (
        rotate_pairs(query_pre, cosine_table, sine_table)
        .astype(jnp.bfloat16)
        .reshape(rows, heads_kv, share, HEAD_SIZE)
    )
    keys_roped = rotate_pairs(keyvalue_before_rotation[:, :heads_kv], cosine_table, sine_table)
    kv_send = (
        jnp.concatenate([keys_roped, keyvalue_before_rotation[:, heads_kv:]], axis=1)
        .astype(jnp.bfloat16)
        .reshape(rows, 2 * heads_kv * HEAD_SIZE)
    )
    start_state = (
        jnp.full((rows, heads_kv, share), -1e30, jnp.float32),
        jnp.zeros((rows, heads_kv, share), jnp.float32),
        jnp.zeros((rows, heads_kv, share, HEAD_SIZE), jnp.float32),
    )
    fold_one = forward_fold(queries, token_pos, scale)
    state = fold_one(
        start_state,
        (
            lax.all_gather(kv_send, "ctx", axis=0, tiled=True),
            lax.all_gather(token_pos, "ctx", axis=0, tiled=True),
        ),
        jnp.int32(0),
    )
    running_max, running_total, running_acc = state
    attended = running_acc / running_total[..., None]
    log_total = running_max + jnp.log(running_total)
    att_low = attended.astype(jnp.bfloat16).reshape(rows, heads_kv * share * HEAD_SIZE)
    mid = inputs + jnp.dot(att_low, out_full, preferred_element_type=jnp.float32)
    gain_two, gate_full, up_full, down_full = (
        lax.all_gather(norm2_gain, "fsdp", axis=0, tiled=True),
        lax.all_gather(w_gate, "fsdp", axis=0, tiled=True),
        lax.all_gather(w_up, "fsdp", axis=0, tiled=True),
        lax.all_gather(w_down, "fsdp", axis=1, tiled=True),
    )
    normed_two, factor_two = normalize(mid, gain_two.astype(jnp.float32))
    act_two = normed_two.astype(jnp.bfloat16)
    gate = jnp.dot(act_two, gate_full, preferred_element_type=jnp.float32)
    up_part = jnp.dot(act_two, up_full, preferred_element_type=jnp.float32)
    sigma = jax.nn.sigmoid(gate)
    swish = gate * sigma
    hidden = (swish * up_part).astype(jnp.bfloat16)
    result = mid + jnp.dot(hidden, down_full, preferred_element_type=jnp.float32)
    grad_y = cotangent[0].astype(jnp.float32)
    grad_y_low = grad_y.astype(jnp.bfloat16)
    gain_two_b, gate_back, up_back, down_back = (
        lax.all_gather(norm2_gain, "fsdp", axis=0, tiled=True),
        lax.all_gather(w_gate, "fsdp", axis=0, tiled=True),
        lax.all_gather(w_up, "fsdp", axis=0, tiled=True),
        lax.all_gather(w_down, "fsdp", axis=1, tiled=True),
    )
    grad_down = jnp.einsum("tf,td->fd", hidden, grad_y_low, preferred_element_type=jnp.float32)
    grad_hidden = jnp.einsum("td,fd->tf", grad_y_low, down_back, preferred_element_type=jnp.float32)
    grad_gate_pre = (grad_hidden * up_part * sigma * (1.0 + gate * (1.0 - sigma))).astype(
        jnp.bfloat16
    )
    grad_up_pre = (grad_hidden * swish).astype(jnp.bfloat16)
    grad_gate = jnp.einsum("td,tf->df", act_two, grad_gate_pre, preferred_element_type=jnp.float32)
    grad_up = jnp.einsum("td,tf->df", act_two, grad_up_pre, preferred_element_type=jnp.float32)
    grad_act_two = jnp.einsum(
        "tf,df->td", grad_gate_pre, gate_back, preferred_element_type=jnp.float32
    )
    grad_act_two = grad_act_two + jnp.einsum(
        "tf,df->td", grad_up_pre, up_back, preferred_element_type=jnp.float32
    )
    grad_mid_norm, grad_gain_two = norm_back(
        mid, factor_two, gain_two_b.astype(jnp.float32), grad_act_two
    )
    grad_mid = grad_y + grad_mid_norm
    gain_one_b, query_back, keyvalue_back, out_back = (
        lax.all_gather(norm1_gain, "fsdp", axis=0, tiled=True),
        lax.all_gather(w_query, "fsdp", axis=0, tiled=True),
        lax.all_gather(keyvalue_projection, "fsdp", axis=0, tiled=True),
        lax.all_gather(w_out, "fsdp", axis=1, tiled=True),
    )
    grad_mid_low = grad_mid.astype(jnp.bfloat16)
    grad_outw = jnp.einsum("tc,td->cd", att_low, grad_mid_low, preferred_element_type=jnp.float32)
    grad_att = (
        jnp.einsum("td,cd->tc", grad_mid_low, out_back, preferred_element_type=jnp.float32)
        .astype(jnp.bfloat16)
        .reshape(rows, heads_kv, share, HEAD_SIZE)
    )
    delta = jnp.sum(grad_att.astype(jnp.float32) * attended, axis=-1)
    query_zero = jnp.zeros((rows, heads_kv, share, HEAD_SIZE), jnp.float32)
    back_state = (query_zero, jnp.zeros((sequence_length, 2, heads_kv, HEAD_SIZE), jnp.float32))
    fold_two = backward_fold(queries, token_pos, log_total, grad_att, delta, scale)
    back_result = fold_two(
        back_state,
        (
            lax.all_gather(kv_send, "ctx", axis=0, tiled=True),
            lax.all_gather(token_pos, "ctx", axis=0, tiled=True),
        ),
        jnp.int32(0),
    )
    grad_q = back_result[0]
    grad_kv = (
        lax.psum_scatter(
            back_result[1].reshape(sequence_length, 2 * heads_kv * HEAD_SIZE).astype(jnp.bfloat16),
            "ctx",
            scatter_dimension=0,
            tiled=True,
        )
        .astype(jnp.float32)
        .reshape(rows, 2 * heads_kv, HEAD_SIZE)
    )
    grad_keys_pre = unrotate(grad_kv[:, :heads_kv], cosine_table, sine_table)
    grad_kv_pre = (
        jnp.concatenate([grad_keys_pre, grad_kv[:, heads_kv:]], axis=1)
        .astype(jnp.bfloat16)
        .reshape(rows, 2 * heads_kv * HEAD_SIZE)
    )
    grad_q_pre = (
        unrotate(grad_q.reshape(rows, heads_kv * share, HEAD_SIZE), cosine_table, sine_table)
        .astype(jnp.bfloat16)
        .reshape(rows, heads_kv * share * HEAD_SIZE)
    )
    grad_query = jnp.einsum(
        "td,tc->dc", first_activation, grad_q_pre, preferred_element_type=jnp.float32
    )
    grad_keyvalue = jnp.einsum(
        "td,tc->dc", first_activation, grad_kv_pre, preferred_element_type=jnp.float32
    )
    grad_act_one = jnp.einsum(
        "tc,dc->td", grad_q_pre, query_back, preferred_element_type=jnp.float32
    )
    grad_act_one = grad_act_one + jnp.einsum(
        "tc,dc->td", grad_kv_pre, keyvalue_back, preferred_element_type=jnp.float32
    )
    grad_in_norm, grad_gain_one = norm_back(
        inputs, factor_one, gain_one_b.astype(jnp.float32), grad_act_one
    )
    input_grad = grad_mid + grad_in_norm
    shards = (
        lax.psum_scatter(
            grad_gain_one.astype(jnp.bfloat16), "fsdp", scatter_dimension=0, tiled=True
        ).astype(jnp.float32),
        lax.psum_scatter(
            grad_query.astype(jnp.bfloat16), "fsdp", scatter_dimension=0, tiled=True
        ).astype(jnp.float32),
        lax.psum_scatter(
            grad_keyvalue.astype(jnp.bfloat16), "fsdp", scatter_dimension=0, tiled=True
        ).astype(jnp.float32),
        lax.psum_scatter(
            grad_outw.astype(jnp.bfloat16), "fsdp", scatter_dimension=1, tiled=True
        ).astype(jnp.float32),
        lax.psum_scatter(
            grad_gain_two.astype(jnp.bfloat16), "fsdp", scatter_dimension=0, tiled=True
        ).astype(jnp.float32),
        lax.psum_scatter(
            grad_gate.astype(jnp.bfloat16), "fsdp", scatter_dimension=0, tiled=True
        ).astype(jnp.float32),
        lax.psum_scatter(
            grad_up.astype(jnp.bfloat16), "fsdp", scatter_dimension=0, tiled=True
        ).astype(jnp.float32),
        lax.psum_scatter(
            grad_down.astype(jnp.bfloat16), "fsdp", scatter_dimension=1, tiled=True
        ).astype(jnp.float32),
    )
    totals = (
        lax.psum(shards[0].astype(jnp.bfloat16), "ctx").astype(jnp.float32),
        lax.psum(shards[1].astype(jnp.bfloat16), "ctx").astype(jnp.float32),
        lax.psum(shards[2].astype(jnp.bfloat16), "ctx").astype(jnp.float32),
        lax.psum(shards[3].astype(jnp.bfloat16), "ctx").astype(jnp.float32),
        lax.psum(shards[4].astype(jnp.bfloat16), "ctx").astype(jnp.float32),
        lax.psum(shards[5].astype(jnp.bfloat16), "ctx").astype(jnp.float32),
        lax.psum(shards[6].astype(jnp.bfloat16), "ctx").astype(jnp.float32),
        lax.psum(shards[7].astype(jnp.bfloat16), "ctx").astype(jnp.float32),
    )
    return (
        result.astype(jnp.bfloat16)[None],
        input_grad[None],
        totals[0],
        totals[1],
        totals[2],
        totals[3],
        totals[4],
        totals[5],
        totals[6],
        totals[7],
    )


def solution(mesh):
    return jax.shard_map(
        local,
        mesh=mesh,
        in_specs=(
            P("fsdp", "ctx", None),
            P("fsdp", "ctx"),
            P("fsdp"),
            P("fsdp", None),
            P("fsdp", None),
            P(None, "fsdp"),
            P("fsdp"),
            P("fsdp", None),
            P("fsdp", None),
            P(None, "fsdp"),
            P("fsdp", "ctx", None),
        ),
        out_specs=(
            P("fsdp", "ctx", None),
            P("fsdp", "ctx", None),
            P("fsdp"),
            P("fsdp", None),
            P("fsdp", None),
            P(None, "fsdp"),
            P("fsdp"),
            P("fsdp", None),
            P("fsdp", None),
            P(None, "fsdp"),
        ),
        check_vma=False,
    )
```

profile of v0, /device:TPU:23, one launch (start us, length us, event | category | flops | bytes accessed | tf_op | source)
XLA Modules:
  0.0 1026.1 jit_solution(14021774586654012809)
XLA Ops:
  12.7 15.7 %all-reduce.10 = (bf16[576]{0:T(1024)(128)(2,1)S(1)}, bf16[576]{0:T(1024)(128)(2,1)S(1)}) all-reduce(bf16[576]{0:T(1024)(128)(2,1)S(1)} %dynamic-update-slice, bf16[576]{0:T(1024)(128)(2,1)S(1)} %dynamic-update-slice.1), channel_id=1, replica_groups=mesh['fsdp'=8,'ctx'=16] {'fsdp'}, use_global_device_ids=true, to_apply=%add | all-reduce | flops 1152 | bytes 4608
  28.4 29.0 %all_gather.42 = bf16[576,384]{1,0:T(8,128)(2,1)S(1)} all-gather(bf16[72,384]{1,0:T(8,128)(2,1)} %param.19), channel_id=1, replica_groups=mesh['fsdp'=8,'ctx'=16] {'fsdp'}, dimensions={0}, use_global_device_ids=true | all-gather | bytes 497664 | tf_op jit(solution)/shard_map/all_gather | solution.py:173
  62.2 27.0 %all-gather = s32[1,4096]{1,0:T(1,128)S(1)} all-gather(s32[1,256]{1,0:T(1,128)S(1)} %copy-done.19), channel_id=2, replica_groups=mesh['fsdp'=8,'ctx'=16] {'ctx'}, dimensions={1}, use_global_device_ids=true | all-gather | bytes 17408 | tf_op jit(solution)/shard_map/all_gather | solution.py:205
  90.4 32.4 %all_gather.44 = bf16[576,576]{1,0:T(8,128)(2,1)} all-gather(bf16[72,576]{1,0:T(8,128)(2,1)S(1)} %copy-done.20), channel_id=1, replica_groups=mesh['fsdp'=8,'ctx'=16] {'fsdp'}, dimensions={0}, use_global_device_ids=true | all-gather | bytes 746496 | tf_op jit(solution)/shard_map/all_gather | solution.py:172
  122.9 30.9 %all_gather.45 = bf16[576,576]{0,1:T(8,128)(2,1)S(1)} all-gather(bf16[576,72]{0,1:T(8,128)(2,1)S(1)} %copy-done.21), channel_id=1, replica_groups=mesh['fsdp'=8,'ctx'=16] {'fsdp'}, dimensions={1}, use_global_device_ids=true | all-gather | bytes 746496 | tf_op jit(solution)/shard_map/all_gather | solution.py:174
  163.6 48.6 %while.28 = (s32[]{:T(128)}, f32[256,3,3]{0,2,1:T(4,128)S(1)}, f32[256,3,3]{0,2,1:T(4,128)S(1)}, f32[256,3,3,64]{0,3,2,1:T(8,128)S(1)}, s32[16,256]{1,0:T(8,128)...) while((s32[]{:T(128)}, f32[256,3,3]{0,2,1:T(4,128)S(1)}, ...), condition=%wide.region_4.5_spmd.clone, body=%wide.region_1.4_spmd.clone.sunk | while | flops 159182080 | bytes 9562241 | solution.py:85
  213.9 3.4 fusion.68
  217.3 6.6 all-gather.8.cloned.1.call-done
  223.9 3.4 fusion.67
  227.4 50.0 %all-gather.12.cloned.1.call-done = bf16[1536,576]{0,1:T(8,128)(2,1)} async-done(((bf16[1536,72]{0,1:T(8,128)(2,1)}), bf16[1536,576]{0,1:T(8,128)(2,1)}) %all-gather.12.cloned.1.call-update) | async-done | bytes 1769488 | tf_op jit(solution)/shard_map/all_gather | solution.py:218
  277.4 4.8 multiply_convert_fusion
  289.4 3.4 broadcast_in_dim.63
  292.8 112.5 %while.29 = (s32[]{:T(128)}, f32[256,3,3,64]{0,3,2,1:T(8,128)S(1)}, f32[4096,2,3,64]{0,3,2,1:T(8,128)}, bf16[16,256,2,3,64]{1,4,3,2,0:T(8,128)(2,1)}, s32[16,256...) while((s32[]{:T(128)}, f32[256,3,3,64]{0,3,2,1:T(8,128)S(1)}, ...), condition=%wide.region_9.10_spmd.clone, body=%wide.region_8.9_spmd.clone.sunk | while | flops 384139264 | bytes 15471845 | solution.py:141
  408.9 3.1 convolution_convert_fusion.1
  414.0 60.4 %reduce-scatter.22.cloned.1.call-done = bf16[72,576]{1,0:T(8,128)(2,1)} async-done(((bf16[576,576]{1,0:T(8,128)(2,1)}), bf16[72,576]{1,0:T(8,128)(2,1)}) %reduce-scatter.22.cloned.1.call-update) | async-done | bytes 82960
  474.4 78.5 %reduce-scatter.20.cloned.1.call-done = bf16[1536,72]{0,1:T(8,128)(2,1)} async-done(((bf16[1536,576]{0,1:T(8,128)(2,1)}), bf16[1536,72]{0,1:T(8,128)(2,1)}) %reduce-scatter.20.cloned.1.call-update) | async-done | bytes 221200 | tf_op jit(solution)/shard_map/reduce_scatter | solution.py:339
  552.9 77.6 %reduce-scatter.18.cloned.1.call-done = bf16[72,1536]{1,0:T(8,128)(2,1)} async-done(((bf16[576,1536]{1,0:T(8,128)(2,1)}), bf16[72,1536]{1,0:T(8,128)(2,1)}) %reduce-scatter.18.cloned.1.call-update) | async-done | bytes 221200 | tf_op jit(solution)/shard_map/reduce_scatter | solution.py:336
  630.5 77.6 %reduce-scatter.16.cloned.1.call-done = bf16[72,1536]{1,0:T(8,128)(2,1)} async-done(((bf16[576,1536]{1,0:T(8,128)(2,1)}), bf16[72,1536]{1,0:T(8,128)(2,1)}) %reduce-scatter.16.cloned.1.call-update) | async-done | bytes 221200 | tf_op jit(solution)/shard_map/reduce_scatter | solution.py:333
  708.2 4.9 convert_element_type.211
  716.7 112.5 %all-reduce.13.cloned.1.call-done = (bf16[72,576]{1,0:T(8,128)(2,1)}, bf16[576,72]{0,1:T(8,128)(2,1)}, bf16[72,1536]{1,0:T(8,128)(2,1)}, bf16[72,1536]{1,0:T(8,128)(2,1)}, bf16[1536,72]{0,1:T(8,128)(2,1)}) async-done(((bf16[72,576]{1,0:T(8,128)(2,1)}, bf16[576,72]{0,1:T(8,128)(2,1)}, bf16[72,1536]{1,0:T(8,128)(2,1)}, bf16[72,1536]{1,0:T(8,128)(2,1)}, bf16[1536,72]{0,1:T(8,128)(2,1)}), ...) | async-done | bytes 829456 | tf_op jit(solution)/shard_map/psum | solution.py:345
  837.7 56.9 %reduce-scatter.14.cloned.1.call-done = bf16[256,384]{0,1:T(8,128)(2,1)} async-done(((bf16[4096,384]{0,1:T(8,128)(2,1)}), bf16[256,384]{0,1:T(8,128)(2,1)}) %reduce-scatter.14.cloned.1.call-update) | async-done | bytes 196624 | tf_op jit(solution)/shard_map/reduce_scatter | solution.py:281
  898.5 15.4 %all-reduce.9 = (bf16[576]{0:T(1024)(128)(2,1)S(1)}, bf16[576]{0:T(1024)(128)(2,1)S(1)}) all-reduce(bf16[576]{0:T(1024)(128)(2,1)S(1)} %get-tuple-element.220, bf16[576]{0:T(1024)(128)(2,1)S(1)} %get-tuple-element.218), channel_id=4, replica_groups=mesh['fsdp'=8,'ctx'=16] {'fsdp'}, use_global_device_ids=true, to_apply=%region_13.14.clone | all-reduce | flops 1152 | bytes 4608
  915.1 52.7 %reduce-scatter.24.cloned.1.call-done = bf16[72,384]{1,0:T(8,128)(2,1)} async-done(((bf16[576,384]{1,0:T(8,128)(2,1)}), bf16[72,384]{1,0:T(8,128)(2,1)}) %reduce-scatter.24.cloned.1.call-update) | async-done | bytes 55312
  967.9 49.8 %all-reduce.7 = (bf16[72]{0:T(256)(128)(2,1)S(1)}, bf16[72,384]{1,0:T(8,128)(2,1)S(1)}, bf16[72]{0:T(256)(128)(2,1)S(1)}) all-reduce(bf16[72]{0:T(256)(128)(2,1)S(1)} %dynamic-slice.3, bf16[72,384]{1,0:T(8,128)(2,1)} %reduce-scatter.24.cloned.1.call-done, bf16[72]{0:T(256)(128)(2,1)S(1)} %dynamic-slice.11), channel_id=1, replica_groups=mesh['fsdp'=8,'ctx'=16] {'ctx'}, use_global_device_ids=true, to_apply=%region_14.15 | all-reduce | flops 27792 | bytes 111168 | tf_op jit(solution)/shard_map/psum | solution.py:344
  (443 shorter events, 201.9 us)
Async XLA Ops:
  7.2 150.6 %all-gather.6.cloned.1.call-start = ((), (), s32[]{:S(2)}) async-start(), calls=%async_computation.7 | async-start | bytes 3342336 | tf_op jit(solution)/shard_map/all_gather | solution.py:204
  9.0 53.2 %copy-start.19 = (s32[1,256]{1,0:T(1,128)S(1)}, s32[1,256]{1,0:T(1,128)}, u32[]{:S(2)}) copy-start(s32[1,256]{1,0:T(1,128)} %param.16) | copy-start | bytes 3076
  9.0 81.4 %copy-start.20 = (bf16[72,576]{1,0:T(8,128)(2,1)S(1)}, bf16[72,576]{1,0:T(8,128)(2,1)}, u32[]{:S(2)}) copy-start(bf16[72,576]{1,0:T(8,128)(2,1)} %param.18) | copy-start | bytes 248836
  57.4 65.5 %copy-start.21 = (bf16[576,72]{0,1:T(8,128)(2,1)S(1)}, bf16[576,72]{0,1:T(8,128)(2,1)}, u32[]{:S(2)}) copy-start(bf16[576,72]{0,1:T(8,128)(2,1)} %param.20) | copy-start | bytes 248836
  59.3 96.8 %copy-start = (bf16[1,256,576]{1,2,0:T(8,128)(2,1)S(1)}, bf16[1,256,576]{1,2,0:T(8,128)(2,1)}, u32[]{:S(2)}) copy-start(bf16[1,256,576]{1,2,0:T(8,128)(2,1)} %param.15) | copy-start | bytes 884740
  60.1 153.8 %all-gather.10.cloned.1.call-start = ((), (), s32[]{:S(2)}) async-start(), calls=%async_computation.9 | async-start | bytes 1990656 | tf_op jit(solution)/shard_map/all_gather | solution.py:217
  60.8 163.1 %all-gather.8.cloned.1.call-start = ((), (), s32[]{:S(2)}) async-start(), calls=%async_computation.8 | async-start | bytes 1990656 | tf_op jit(solution)/shard_map/all_gather | solution.py:216
  61.6 215.8 %all-gather.12.cloned.1.call-start = ((), (), s32[]{:S(2)}) async-start(), calls=%async_computation.10 | async-start | bytes 1990656 | tf_op jit(solution)/shard_map/all_gather | solution.py:218
  62.1 351.8 %reduce-scatter.26.cloned.1.call-start = ((), (), s32[]{:S(2)}) async-start(), calls=%async_computation.17 | async-start | bytes 829440
  217.3 60.1 %copy-start.15 = (bf16[1,256,576]{1,2,0:T(8,128)(2,1)S(1)}, bf16[1,256,576]{1,2,0:T(8,128)(2,1)}, u32[]{:S(2)}) copy-start(bf16[1,256,576]{1,2,0:T(8,128)(2,1)} %param.25) | copy-start | bytes 884740
  277.4 4.8 copy-start.1
  289.1 185.3 %reduce-scatter.22.cloned.1.call-start = ((), (), s32[]{:S(2)}) async-start(), calls=%async_computation.15 | async-start | bytes 829440
  289.4 3.4 copy-start.18
  405.4 3.3 copy-start.12
  406.8 146.1 %reduce-scatter.20.cloned.1.call-start = ((), (), s32[]{:S(2)}) async-start(), calls=%async_computation.14 | async-start | bytes 1990656 | tf_op jit(solution)/shard_map/reduce_scatter | solution.py:339
  408.8 3.2 copy-start.8
  408.8 221.7 %reduce-scatter.18.cloned.1.call-start = ((), (), s32[]{:S(2)}) async-start(), calls=%async_computation.13 | async-start | bytes 1990656 | tf_op jit(solution)/shard_map/reduce_scatter | solution.py:336
  412.0 296.1 %reduce-scatter.16.cloned.1.call-start = ((), (), s32[]{:S(2)}) async-start(), calls=%async_computation.12 | async-start | bytes 1990656 | tf_op jit(solution)/shard_map/reduce_scatter | solution.py:333
  413.9 415.3 %all-reduce.13.cloned.1.call-start = ((), (), s32[]{:S(2)}) async-start(), calls=%async_computation.18 | async-start | bytes 1695744 | tf_op jit(solution)/shard_map/psum | solution.py:345
  708.1 186.5 %reduce-scatter.14.cloned.1.call-start = ((), (), s32[]{:S(2)}) async-start(), calls=%async_computation.11 | async-start | bytes 3342336 | tf_op jit(solution)/shard_map/reduce_scatter | solution.py:281
  713.1 254.7 %reduce-scatter.24.cloned.1.call-start = ((), (), s32[]{:S(2)}) async-start(), calls=%async_computation.16 | async-start | bytes 497664
  832.3 65.3 %copy-start.5 = (bf16[576,384]{1,0:T(8,128)(2,1)S(1)}, bf16[576,384]{1,0:T(8,128)(2,1)}, u32[]{:S(2)}) copy-start(bf16[576,384]{1,0:T(8,128)(2,1)} %copy-done.4) | copy-start | bytes 1327108
  835.9 62.1 %copy-start.3 = (bf16[576,576]{1,0:T(8,128)(2,1)S(1)}, bf16[576,576]{1,0:T(8,128)(2,1)}, u32[]{:S(2)}) copy-start(bf16[576,576]{1,0:T(8,128)(2,1)} %all_gather.44) | copy-start | bytes 1990660
  835.9 62.1 %copy-start.13 = (bf16[256,9,64]{0,2,1:T(8,128)(2,1)S(1)}, bf16[256,9,64]{0,2,1:T(8,128)(2,1)}, u32[]{:S(2)}) copy-start(bf16[256,9,64]{0,2,1:T(8,128)(2,1)} %copy-done.12) | copy-start | bytes 884740
  (10 other events, 17.9 us)
Sparse Core Ops, SparseCore 0:
  60.2 54.2 all-gather.5
  116.8 53.9 all-gather.9
  173.1 50.7 all-gather.7
  226.1 51.2 all-gather.11
  289.2 67.3 reduce-scatter.25
  407.0 67.4 reduce-scatter.21
  478.2 74.6 reduce-scatter.19
  556.7 73.7 reduce-scatter.17
  634.3 73.7 reduce-scatter.15
  710.8 118.3 all-reduce.12
  831.7 62.7 reduce-scatter.13
  898.5 69.3 reduce-scatter.23
where the time goes:
time: 1040 us; the launch traced here: 1030 us
  waiting for transfers between devices  575 us (55%)
  blocking collectives  200 us (19%)
  matrix products  97.9 us (9%)
  other arithmetic  65.5 us (6%)
  local copies, waits for them, and re-layouts  58.9 us (6%)
  between operations  16 us (2%)
  loops' own time  12.1 us (1%)
    unnamed x15, waiting for transfers between devices  115 us
    psum x1, waiting for transfers between devices, local(): lax.psum(shards[1].astype(jnp.bfloat16), 'ctx').astype(jnp.float32)  113 us
    reduce_scatter x1, waiting for transfers between devices, local(): lax.psum_scatter(grad_down.astype(jnp.bfloat16), 'fsdp', scatter_dimensio...  78.5 us
    reduce_scatter x1, waiting for transfers between devices, local(): lax.psum_scatter(grad_gate.astype(jnp.bfloat16), 'fsdp', scatter_dimensio...  77.6 us
    reduce_scatter x1, waiting for transfers between devices, local(): lax.psum_scatter(grad_up.astype(jnp.bfloat16), 'fsdp', scatter_dimension=...  77.6 us
    reduce_scatter x1, waiting for transfers between devices, local(): lax.psum_scatter(back_result[1].reshape(sequence_length, 2 * heads_kv * H...  56.9 us
    all_gather x1, waiting for transfers between devices, local(): lax.all_gather(w_down, 'fsdp', axis=1, tiled=True)  50 us
    psum x1, blocking collectives, local(): lax.psum(shards[0].astype(jnp.bfloat16), 'ctx').astype(jnp.float32)  49.8 us
  transfers between devices with their start and end apart: 12, of which 9 were waited for; matrix products, arithmetic and copies ran while one was open for 19% of the time, Pallas kernels for 0%

commit v1 on v0

v1 whole, which is shorter than its diff:
```python
import numpy as np

import jax
import jax.numpy as jnp
from jax import lax
from jax.experimental import pallas as pl
from jax.experimental.pallas import tpu as pltpu
from jax.sharding import PartitionSpec as P

MESH = pl.DeviceIdType.MESH
BF = jnp.bfloat16
F32 = jnp.float32
D = 576
DP = 640
ROWS = 256
WA = 512
WB = 2816
FC = 256
NEG = -1e30
STEPS = (0, 1, 3, 2)
BACK = (2, 1, 3, 0)


def mm(a, b):
    return jnp.dot(a, b, preferred_element_type=F32)


def mm_nt(a, b):
    return lax.dot_general(a, b, (((1,), (1,)), ((), ())), preferred_element_type=F32)


def mm_tn(a, b):
    return lax.dot_general(a, b, (((0,), (0,)), ((), ())), preferred_element_type=F32)


def lane_iota(shape):
    return lax.broadcasted_iota(jnp.int32, shape, len(shape) - 1)


def partner_lanes(u):
    lane = lane_iota(u.shape)
    return jnp.where(lane % 64 < 32, pltpu.roll(u, 96, 1), pltpu.roll(u, 32, 1))


def kernel(
    xc, wa_in, wb_in, cos_in, sin_in,
    bo_out, ig_out, ga_out, gb_out,
    xc_r, wa, wb, cos_s, sin_s, kv, bias, perm,
    qt, qx, dot_, dox, st_m, st_l, acc, ot, dqt,
    xs, dy, mid, act1, act1t, attb, dmid,
    dkv_p, d1_r, d2_s, d2_r,
    ga, gac, gbc, gax, gbx, ga2, gb2, gaz, gbz, ga3, gb3, gal, gbl, ga4, gb4, gay, gby,
    gaf, gbf, bo_s, bo_r, ig_s, ig_r,
    ss, rs, ls,
):
    f = lax.axis_index("fsdp")
    c = lax.axis_index("ctx")
    zh, xx = f // 4, f % 4
    zl, yy, k = c // 8, (c // 2) % 4, c % 2
    fz = (1 - zh) * 4 + xx

    def ctx_at(z, y, core):
        return z * 8 + y * 2 + core

    def slot_at(z, y, core):
        return y * 4 + z * 2 + core

    other = ctx_at(zl, yy, 1 - k)
    sends = []
    used = [0]

    def take(n):
        used[0] += n
        return used[0] - n

    def remote(src, dst, sem, fs, cs):
        return pltpu.make_async_remote_copy(
            src_ref=src, dst_ref=dst, send_sem=ss.at[sem], recv_sem=rs.at[sem],
            device_id={"fsdp": fs, "ctx": cs}, device_id_type=MESH,
        )

    def send(src, dst, sem, fs, cs):
        copy = remote(src, dst, sem, fs, cs)
        copy.start()
        sends.append(copy)
        return copy

    def arrived(dst, sem):
        remote(dst, dst, sem, f, other).wait_recv()

    barrier = pltpu.get_barrier_semaphore()
    for step in range(1, 16):
        pl.semaphore_signal(
            barrier, inc=1, device_id={"fsdp": f, "ctx": (c + step) % 16}, device_id_type=MESH
        )
    pl.semaphore_signal(barrier, inc=1, device_id={"fsdp": fz, "ctx": c}, device_id_type=MESH)
    for step in range(1, 4):
        pl.semaphore_signal(
            barrier, inc=1, device_id={"fsdp": zh * 4 + (xx + step) % 4, "ctx": c},
            device_id_type=MESH,
        )
    pl.semaphore_wait(barrier, 19)

    sem_x = take(16)
    for step in range(1, 16):
        send(xc.at[(c + step) % 16], xc_r.at[c], sem_x + step, f, (c + step) % 16)
    local = [
        pltpu.make_async_copy(xc.at[c], xc_r.at[c], ls.at[0]),
        pltpu.make_async_copy(wa_in.at[k], wa.at[k, f], ls.at[1]),
        pltpu.make_async_copy(wb_in.at[k], wb.at[k, f], ls.at[2]),
        pltpu.make_async_copy(cos_in.at[:, c], cos_s, ls.at[3]),
        pltpu.make_async_copy(sin_in.at[:, c], sin_s, ls.at[4]),
    ]
    for copy in local:
        copy.start()

    def gather_first(w_in, w, sem):
        send(w_in.at[k], w.at[k, f], sem, fz, c)
        for step in range(1, 4):
            send(w_in.at[k], w.at[k, f], sem + step, zh * 4 + (xx + step) % 4, c)

    def gather_second(w, sem):
        arrived(w.at[k, fz], sem)
        return [
            send(w.at[k, fz], w.at[k, fz], sem + 3 + step, zh * 4 + (xx + step) % 4, c)
            for step in range(1, 4)
        ]

    def gather_third(w, sem):
        for step in range(1, 4):
            from_x = (xx + 4 - step) % 4
            arrived(w.at[k, zh * 4 + from_x], sem + step)
            arrived(w.at[k, (1 - zh) * 4 + from_x], sem + 3 + step)
        return [send(w.at[k], w.at[k], sem + 7, f, other)]

    def gather_last(w, sem):
        arrived(w.at[1 - k], sem + 7)

    sem_a = take(8)
    sem_b = take(8)
    gather_first(wa_in, wa, sem_a)
    gather_first(wb_in, wb, sem_b)

    def make_bias(slot, carry):
        e = ctx_at((slot // 2) % 2, slot // 4, slot % 2)
        j = lax.broadcasted_iota(jnp.int32, (128, 128), 0)
        i = lax.broadcasted_iota(jnp.int32, (128, 128), 1)
        ok = (j // 8 < i // 8) | ((j // 8 == i // 8) & (8 * e + j % 8 <= 8 * c + i % 8))
        bias[pl.ds(pl.multiple_of(slot * 128, 128), 128), :] = jnp.where(ok, 0.0, NEG)
        return carry

    lax.fori_loop(0, 16, make_bias, 0)
    gather_second(wa, sem_a)
    for copy in local:
        copy.wait()
    for step in range(1, 16):
        arrived(xc_r.at[(c + 16 - step) % 16], sem_x + step)

    x_raw = xc_r[:, 0:16, :].reshape(ROWS, DP)
    lane = lane_iota((ROWS, DP))
    tag = jnp.sum(jnp.where(lane == 72, x_raw.astype(F32), 0.0), axis=1, keepdims=True)
    place = lane_iota((ROWS, ROWS)).astype(F32)
    perm[...] = jnp.where(tag == place, 1.0, 0.0).astype(BF)
    perm_t = jnp.where(tag == place, 1.0, 0.0).T.astype(BF)
    x = mm(perm_t, x_raw)
    x = jnp.where(lane % 80 < 72, x, 0.0)
    xs[...] = x
    dy[...] = mm(perm_t, xc_r[:, 16:32, :].reshape(ROWS, DP)).astype(BF)

    gather_third(wa, sem_a)
    r1 = lax.rsqrt(jnp.sum(x * x, axis=-1, keepdims=True) * (1.0 / D) + 1e-5)
    gather_last(wa, sem_a)

    def gain_row(which):
        hot = jnp.where(lane_iota((16, 128)) == 64 + which, 1.0, 0.0).astype(BF)
        block = wa[1, :, :, 0:128].reshape(DP, 128)
        return mm_nt(hot, block)[0:1, :]

    gain1, gain2 = gain_row(0), gain_row(1)
    a1 = x * r1 * gain1
    a1b = a1.astype(BF)
    act1[...] = a1b
    act1t[...] = a1.T.astype(BF)

    cos = cos_s[...].reshape(ROWS, 128)
    sin = sin_s[...].reshape(ROWS, 128)
    low = lane_iota((ROWS, 128)) < 64
    cos_kv = jnp.where(low, cos, 1.0)
    sin_kv = jnp.where(low, sin, 0.0)

    mine = slot_at(zl, yy, k)
    kv_pre = mm(a1b, wa[1, :, :, 128:512].reshape(DP, 384))
    for g in range(3):
        u = kv_pre[:, 128 * g : 128 * g + 128]
        kv[mine, g] = (u * cos_kv + partner_lanes(u) * sin_kv).astype(BF)
    sem_k = take(16)

    send(kv.at[mine], kv.at[mine], sem_k, f, other)
    for off in STEPS:
        for a in (0, 1):
            if (a, off) != (0, 0):
                to = ctx_at(zl if a == 0 else 1 - zl, (yy + off) % 4, k)
                send(kv.at[mine], kv.at[mine], sem_k + a * 4 + off, f, to)

    def kv_direct(off):
        for a in (0, 1):
            if (a, off) != (0, 0):
                at = slot_at(zl if a == 0 else 1 - zl, (yy + 4 - off) % 4, k)
                arrived(kv.at[at], sem_k + a * 4 + off)
                send(kv.at[at], kv.at[at], sem_k + 8 + a * 4 + off, f, other)

    def kv_across(off):
        for a in (0, 1):
            at = slot_at(zl if a == 0 else 1 - zl, (yy + 4 - off) % 4, 1 - k)
            arrived(kv.at[at], sem_k if (a, off) == (0, 0) else sem_k + 8 + a * 4 + off)

    for t in range(5):
        w = wa[0, :, :, 128 * t : 128 * t + 128] if t < 4 else wa[1, :, :, 0:128]
        u = mm(a1b, w.reshape(DP, 128))
        u = (u * cos + partner_lanes(u) * sin).astype(BF).astype(F32) * 0.125
        for half in range(2):
            h = 2 * t + half
            if h < 9:
                g, r = h // 3, h % 3
                v = jnp.where(low, u if half == 0 else pltpu.roll(u, 64, 1), 0.0)
                vt = v.T
                for ih in range(2):
                    at = 384 * ih + 128 * r
                    qx[g, at : at + 128, :] = v[128 * ih : 128 * ih + 128].astype(BF)
                    qt[g, :, at : at + 128] = vt[:, 128 * ih : 128 * ih + 128].astype(BF)

    from_wb = gather_second(wb, sem_b)

    st_m[...] = jnp.full(st_m.shape, NEG, F32)
    st_l[...] = jnp.zeros(st_l.shape, F32)
    acc[...] = jnp.zeros(acc.shape, F32)

    def three(b):
        return jnp.concatenate([b, b, b], axis=1)

    def fold_forward(off):
        group = (yy + 4 - off) % 4

        def per_head(g, carry):
            b3 = three(bias[pl.ds(pl.multiple_of(group * 512, 512), 512), :])
            for key_half, lane_half in ((0, 0), (0, 1), (1, 1)):
                at = 384 * lane_half
                rows = kv[pl.ds(group * 4, 4), g, 128 * key_half : 128 * key_half + 128, :]
                rows = rows.reshape(512, 128)
                s = mm(rows, qt[g, :, at : at + 384])
                if key_half == lane_half:
                    s = s + b3
                old = st_m[g, :, at : at + 384]
                new = jnp.maximum(old, jnp.max(s, axis=0, keepdims=True))
                p = jnp.exp(s - new)
                scale = jnp.exp(old - new)
                st_m[g, :, at : at + 384] = new
                st_l[g, :, at : at + 384] = (
                    st_l[g, :, at : at + 384] * scale + jnp.sum(p, axis=0, keepdims=True)
                )
                acc[g, :, at : at + 384] = acc[g, :, at : at + 384] * scale + mm_tn(
                    rows, p.astype(BF)
                )
            return carry

        lax.fori_loop(0, 3, per_head, 0)

    kv_direct(0)
    kv_direct(STEPS[1])
    kv_across(0)
    fold_forward(0)
    kv_direct(STEPS[2])
    kv_across(STEPS[1])
    fold_forward(STEPS[1])
    kv_direct(STEPS[3])
    kv_across(STEPS[2])
    fold_forward(STEPS[2])
    from_wb += gather_third(wb, sem_b)
    kv_across(STEPS[3])
    fold_forward(STEPS[3])

    def head_rows(ref, g, r):
        return jnp.concatenate(
            [ref[g, :, 384 * ih + 128 * r : 384 * ih + 128 * r + 128].T for ih in range(2)], axis=0
        )

    for g in range(3):
        ot[g] = acc[g] / st_l[g]
        st_l[g] = st_m[g] + jnp.log(st_l[g])
    for t in range(5):
        a = pltpu.roll(head_rows(ot, 2 * t // 3, 2 * t % 3), 64, 1)
        b = head_rows(ot, (2 * t + 1) // 3, (2 * t + 1) % 3) if t < 4 else jnp.zeros((ROWS, 128), F32)
        attb[:, 128 * t : 128 * t + 128] = jnp.where(low, a, b).astype(BF)

    gather_last(wb, sem_b)

    def out_t(half):
        if half == 0:
            return wb[0, :, :, 2304:2816].reshape(DP, 512)
        return wb[1, :, :, 2304:2432].reshape(DP, 128)

    m0 = xs[...] + mm_nt(attb[:, 0:512], out_t(0)) + mm_nt(attb[:, 512:640], out_t(1))
    r2 = lax.rsqrt(jnp.sum(m0 * m0, axis=-1, keepdims=True) * (1.0 / D) + 1e-5)
    mid[...] = m0
    a2 = m0 * r2 * gain2
    a2b = a2.astype(BF)
    a2t = a2.T.astype(BF)
    dyb = dy[...]
    dyt = dyb.astype(F32).T.astype(BF)

    for copy in from_wb:
        copy.wait_send()
    sends[:] = [copy for copy in sends if all(copy is not done for done in from_wb)]
    gb = wb

    def ff(j, carry):
        total, dact = carry
        cols = pl.ds(pl.multiple_of(j * FC, FC), FC)
        dcol = pl.ds(pl.multiple_of(1536 + (j % 3) * FC, FC), FC)
        wg = wb[0, :, :, cols].reshape(DP, FC)
        wu = wb[1, :, :, cols].reshape(DP, FC)
        wd = wb[j // 3, :, :, dcol].reshape(DP, FC)
        gate, up = mm(a2b, wg), mm(a2b, wu)
        sig = jax.nn.sigmoid(gate)
        swish = gate * sig
        hid = (swish * up).astype(BF)
        total = total + mm_nt(hid, wd)
        dh = mm(dyb, wd)
        dg = (dh * up * sig * (1.0 + gate * (1.0 - sig))).astype(BF)
        du = (dh * swish).astype(BF)
        gb[j // 3, :, :, dcol] = mm(dyt, hid).astype(BF).reshape(8, 80, FC)
        gb[0, :, :, cols] = mm(a2t, dg).astype(BF).reshape(8, 80, FC)
        gb[1, :, :, cols] = mm(a2t, du).astype(BF).reshape(8, 80, FC)
        dact = dact + mm_nt(dg, wg) + mm_nt(du, wu)
        return total, dact

    zero = jnp.zeros((ROWS, DP), F32)
    total, dact = lax.fori_loop(0, 6, ff, (zero, zero))

    def give_back(value, src, dst, sem):
        src[...] = mm(perm[...], value.astype(BF)).astype(BF).reshape(16, 16, DP)
        for step in range(1, 16):
            send(src.at[(c + step) % 16], dst.at[c], sem + step, f, (c + step) % 16)
        dst[c] = src[c]

    sem_o = take(16)
    sem_i = take(16)
    m0 = mid[...]
    give_back(m0 + total, bo_s, bo_r, sem_o)

    dyf = dyb.astype(F32)
    gain_grad2 = jnp.sum(dact * m0 * r2, axis=0, keepdims=True)
    wgt = dact * gain2
    inner = jnp.sum(wgt * m0, axis=-1, keepdims=True) * (1.0 / D)
    dm = dyf + r2 * wgt - m0 * (r2 * r2 * r2) * inner
    dmid[...] = dm
    dmb = dm.astype(BF)
    dmt = dm.T.astype(BF)

    def reducer(width, parts, core_r, x_r, sum2, z_r, sum3, l_r, sum4, y_r, final):
        sem = take(9)
        half = width // 2
        mine_cols = pl.ds(pl.multiple_of(zl * half, 128), half)
        their_cols = pl.ds(pl.multiple_of((1 - zl) * half, 128), half)

        def one():
            send(parts.at[1 - k], core_r, sem, f, other)

        def two():
            arrived(core_r, sem)
            parts[k] = (parts[k].astype(F32) + core_r[...].astype(F32)).astype(BF)
            for step in range(1, 4):
                to = (xx + step) % 4
                for q in range(2):
                    pair = x_r.at[step - 1, q]
                    send(parts.at[k, q * 4 + to], pair, sem_x2 + 2 * (step - 1) + q, q_f(to), c)

        def three_():
            for step in range(3):
                for q in range(2):
                    arrived(x_r.at[step, q], sem_x2 + 2 * step + q)
            for q in range(2):
                v = parts[k, q * 4 + xx].astype(F32)
                for step in range(3):
                    v = v + x_r[step, q].astype(F32)
                sum2[q] = v.astype(BF)
            send(sum2.at[1 - zh], z_r, sem + 1, fz, c)

        def four():
            arrived(z_r, sem + 1)
            sum3[...] = (sum2[zh].astype(F32) + z_r[...].astype(F32)).astype(BF)
            send(sum3.at[:, their_cols], l_r, sem + 2, f, ctx_at(1 - zl, yy, k))

        def five():
            arrived(l_r, sem + 2)
            sum4[...] = (sum3[:, mine_cols].astype(F32) + l_r[...].astype(F32)).astype(BF)
            for step in range(1, 4):
                send(sum4, y_r.at[step - 1], sem + 2 + step, f, ctx_at(zl, (yy + step) % 4, k))

        def six():
            for step in range(1, 4):
                arrived(y_r.at[step - 1], sem + 2 + step)
            v = sum4[...].astype(F32)
            for step in range(3):
                v = v + y_r[step].astype(F32)
            final[k, :, mine_cols] = v.astype(BF)
            piece = final.at[k, :, mine_cols]
            send(piece, piece, sem + 6, f, ctx_at(1 - zl, yy, k))

        def seven():
            arrived(final.at[k, :, their_cols], sem + 6)
            send(final.at[k], final.at[k], sem + 7, f, other)

        def eight():
            arrived(final.at[1 - k], sem + 7)

        sem_x2 = take(6)

        def q_f(to):
            return zh * 4 + to

        return one, two, three_, four, five, six, seven, eight

    for t in range(5):
        w = wb[0, :, :, 2304 + 128 * t : 2432 + 128 * t] if t < 4 else wb[1, :, :, 2304:2432]
        u = mm(dmb, w.reshape(DP, 128)).astype(BF).astype(F32)
        for half in range(2):
            h = 2 * t + half
            if h < 9:
                g, r = h // 3, h % 3
                v = jnp.where(low, 0.0, u if half == 1 else pltpu.roll(u, 64, 1))
                vt = v.T
                for ih in range(2):
                    at = 384 * ih + 128 * r
                    dox[g, at : at + 128, :] = v[128 * ih : 128 * ih + 128].astype(BF)
                    dot_[g, :, at : at + 128] = vt[:, 128 * ih : 128 * ih + 128].astype(BF)
    gb[0, :, :, 2304:2816] = mm(dmt, attb[:, 0:512]).astype(BF).reshape(8, 80, 512)
    gb[1, :, :, 2304:2432] = mm(dmt, attb[:, 512:640]).astype(BF).reshape(8, 80, 128)
    red_b = reducer(WB, gb, gbc, gbx, gb2, gbz, gb3, gbl, gb4, gby, gbf)
    red_b[0]()
    for g in range(3):
        st_m[g] = jnp.sum(dot_[g].astype(F32) * ot[g], axis=0, keepdims=True)
    dqt[...] = jnp.zeros(dqt.shape, F32)

    def fold_backward(at_step, off):
        group = (yy + 4 - off) % 4

        def per_head(g, carry):
            b3 = three(bias[pl.ds(pl.multiple_of(group * 512, 512), 512), :])
            for key_half in range(2):
                rows = kv[pl.ds(group * 4, 4), g, 128 * key_half : 128 * key_half + 128, :]
                rows = rows.reshape(512, 128)
                grad = None
                for lane_half in range(key_half, 2):
                    at = 384 * lane_half
                    s = mm(rows, qt[g, :, at : at + 384])
                    if key_half == lane_half:
                        s = s + b3
                    p = jnp.exp(s - st_l[g, :, at : at + 384])
                    dp = mm(rows, dot_[g, :, at : at + 384])
                    ds = (p * (dp - st_m[g, :, at : at + 384])).astype(BF)
                    part = mm(ds, qx[g, at : at + 384, :]) + mm(
                        p.astype(BF), dox[g, at : at + 384, :]
                    )
                    grad = part if grad is None else grad + part
                    dqt[g, :, at : at + 384] += mm_tn(rows, ds)
                dkv_p[at_step, :, g, 128 * key_half : 128 * key_half + 128, :] = grad.astype(
                    BF
                ).reshape(4, 128, 128)
            return carry

        lax.fori_loop(0, 3, per_head, 0)

    sem_d = take(12)

    def dkv_first(at_step):
        for z in range(2):
            send(
                dkv_p.at[at_step, 2 * z + 1 - k], d1_r.at[at_step, z], sem_d1 + 2 * at_step + z,
                f, other,
            )

    sem_d1 = take(8)

    def dkv_second(at_step, off):
        for z in range(2):
            arrived(d1_r.at[at_step, z], sem_d1 + 2 * at_step + z)
        for z in range(2):
            d2_s[at_step, z] = (
                dkv_p[at_step, 2 * z + k].astype(F32) + d1_r[at_step, z].astype(F32)
            ).astype(BF)
        for a in (0, 1):
            if (a, off) != (0, 0):
                z = zl if a == 0 else 1 - zl
                send(
                    d2_s.at[at_step, z], d2_r.at[a * 4 + off], sem_d + a * 4 + off,
                    f, ctx_at(z, (yy + 4 - off) % 4, k),
                )

    fold_backward(0, BACK[0])
    dkv_first(0)
    red_b[1]()
    fold_backward(1, BACK[1])
    dkv_first(1)
    dkv_second(0, BACK[0])
    fold_backward(2, BACK[2])
    dkv_first(2)
    dkv_second(1, BACK[1])
    red_b[2]()
    fold_backward(3, BACK[3])
    dkv_first(3)
    dkv_second(2, BACK[2])
    red_b[3]()

    dq_tiles = []
    for t in range(5):
        a = head_rows(dqt, 2 * t // 3, 2 * t % 3)
        if t < 4:
            b = pltpu.roll(head_rows(dqt, (2 * t + 1) // 3, (2 * t + 1) % 3), 64, 1)
        else:
            b = jnp.zeros((ROWS, 128), F32)
        u = jnp.where(low, a, b) * 0.125
        dq_tiles.append((u * cos - partner_lanes(u) * sin).astype(BF))
    dq = jnp.concatenate(dq_tiles, axis=1)
    a1t = act1t[...]
    ga[0] = mm(a1t, dq[:, 0:512]).astype(BF).reshape(8, 80, 512)
    dact1 = mm_nt(dq[:, 0:512], wa[0].reshape(DP, 512)) + mm_nt(
        dq[:, 512:640], wa[1, :, :, 0:128].reshape(DP, 128)
    )
    red_b[4]()
    dkv_second(3, BACK[3])

    for a in (0, 1):
        for off in range(4):
            if (a, off) != (0, 0):
                arrived(d2_r.at[a * 4 + off], sem_d + a * 4 + off)
    for g in range(3):
        u = d2_s[3, zl, g].astype(F32)
        for n in range(1, 8):
            u = u + d2_r[n, g].astype(F32)
        u = (u * cos_kv - partner_lanes(u) * sin_kv).astype(BF)
        at = 128 + 128 * g
        ga[1, :, :, at : at + 128] = mm(a1t, u).astype(BF).reshape(8, 80, 128)
        dact1 = dact1 + mm_nt(u, wa[1, :, :, at : at + 128].reshape(DP, 128))

    x = xs[...]
    gain_grad1 = jnp.sum(dact1 * x * r1, axis=0, keepdims=True)
    gains = jnp.concatenate([gain_grad1, gain_grad2, jnp.zeros((6, DP), F32)], axis=0)
    hot = jnp.where(
        lane_iota((8, 128)) == 64 + lax.broadcasted_iota(jnp.int32, (8, 128), 0), 1.0, 0.0
    )
    hot = jnp.where(lax.broadcasted_iota(jnp.int32, (8, 128), 0) < 2, hot, 0.0)
    gain_cols = mm(gains.T.astype(BF), hot.astype(BF))
    ga[1, :, :, 0:128] = (mm(a1t, dq[:, 512:640]) + gain_cols).astype(BF).reshape(8, 80, 128)
    red_a = reducer(WA, ga, gac, gax, ga2, gaz, ga3, gal, ga4, gay, gaf)
    red_a[0]()

    wgt = dact1 * gain1
    inner = jnp.sum(wgt * x, axis=-1, keepdims=True) * (1.0 / D)
    give_back(
        dmid[...] + r1 * wgt - x * (r1 * r1 * r1) * inner, ig_s, ig_r, sem_i
    )
    red_a[1]()
    red_b[5]()
    red_a[2]()
    red_b[6]()
    red_a[3]()
    red_a[4]()
    red_b[7]()
    gb_out[...] = gbf[...]
    red_a[5]()
    for step in range(1, 16):
        arrived(bo_r.at[(c + 16 - step) % 16], sem_o + step)
    bo_out[...] = bo_r[...]
    red_a[6]()
    for step in range(1, 16):
        arrived(ig_r.at[(c + 16 - step) % 16], sem_i + step)
    ig_out[...] = ig_r[...]
    red_a[7]()
    ga_out[...] = gaf[...]
    for copy in sends:
        copy.wait_send()


def tables():
    freq = np.power(np.float32(100000.0), -(np.arange(32, dtype=np.float32) * np.float32(2.0 / 64)))
    angle = np.arange(4096, dtype=np.float32)[:, None] * freq[None, :].astype(np.float32)
    cos, sin = np.cos(angle), np.sin(angle)
    cos = np.concatenate([cos, cos, cos, cos], axis=1)
    sin = np.concatenate([-sin, sin, -sin, sin], axis=1)
    shape = (32, 16, 8, 128)
    return cos.reshape(shape).astype(np.float32), sin.reshape(shape).astype(np.float32)


def pad_model(rows):
    return jnp.pad(rows.reshape(ROWS, 8, 72), ((0, 0), (0, 0), (0, 8))).reshape(ROWS, DP)


def by_target(rows):
    return rows.reshape(2, 16, 8, DP).transpose(1, 0, 2, 3).reshape(16, 16, DP)


def by_token(rows):
    rows = rows.reshape(16, 2, 8, 8, 80)[..., :72]
    return rows.transpose(1, 0, 2, 3, 4).reshape(1, ROWS, D)


def local(tokens, positions, gain1, wq, wkv, wo, gain2, wg, wu, wd, cotangent):
    place = (positions[0] // 128) * 8 + positions[0] % 8
    x = pad_model(tokens[0])
    x = jnp.where(lane_iota((ROWS, DP)) == 72, place[:, None].astype(BF), x)
    xc = jnp.concatenate([by_target(x), by_target(pad_model(cotangent[0]))], axis=1)
    w_kv = wkv.reshape(72, 2, 3, 64).transpose(0, 2, 1, 3).reshape(72, 384)
    gains = jnp.stack([gain1, gain2], axis=1)
    wa = jnp.concatenate([wq, gains, jnp.zeros((72, 62), BF), w_kv], axis=1)
    wa = jnp.pad(jnp.stack([wa[:, :WA], wa[:, WA:]]), ((0, 0), (0, 8), (0, 0)))
    wot, wdt = wo.T, wd.T
    wb = jnp.stack(
        [
            jnp.concatenate([wg, wdt[:, :768], wot[:, :512]], axis=1),
            jnp.concatenate([wu, wdt[:, 768:], wot[:, 512:], jnp.zeros((72, 448), BF)], axis=1),
        ]
    )
    wb = jnp.pad(wb, ((0, 0), (0, 8), (0, 0)))
    cos, sin = tables()

    def v(shape, dtype=BF):
        return pltpu.VMEM(shape, dtype)

    any_space = pl.BlockSpec(memory_space=pl.ANY)
    vmem = pl.BlockSpec(memory_space=pltpu.VMEM)
    scratch = [
        v((16, 32, DP)), v((2, 8, 80, WA)), v((2, 8, 80, WB)),
        v((32, 8, 128), F32), v((32, 8, 128), F32),
        v((16, 3, 256, 128)), v((2048, 128), F32), v((ROWS, ROWS)),
        v((3, 128, 768)), v((3, 768, 128)), v((3, 128, 768)), v((3, 768, 128)),
        v((3, 1, 768), F32), v((3, 1, 768), F32), v((3, 128, 768), F32), v((3, 128, 768), F32),
        v((3, 128, 768), F32),
        v((ROWS, DP), F32), v((ROWS, DP)), v((ROWS, DP), F32), v((ROWS, DP)), v((DP, ROWS)),
        v((ROWS, DP)), v((ROWS, DP), F32),
        v((4, 4, 3, 256, 128)), v((4, 2, 3, 256, 128)), v((4, 2, 3, 256, 128)),
        v((8, 3, 256, 128)),
        v((2, 8, 80, WA)), v((8, 80, WA)), v((8, 80, WB)),
        v((3, 2, 80, WA)), v((3, 2, 80, WB)), v((2, 80, WA)), v((2, 80, WB)),
        v((80, WA)), v((80, WB)), v((80, WA)), v((80, WB)),
        v((80, WA // 2)), v((80, WB // 2)), v((80, WA // 2)), v((80, WB // 2)),
        v((3, 80, WA // 2)), v((3, 80, WB // 2)), v((2, 80, WA)), v((2, 80, WB)),
        v((16, 16, DP)), v((16, 16, DP)), v((16, 16, DP)), v((16, 16, DP)),
        pltpu.SemaphoreType.DMA((140,)), pltpu.SemaphoreType.DMA((140,)),
        pltpu.SemaphoreType.DMA((5,)),
    ]
    bo, ig, ga, gb = pl.pallas_call(
        kernel,
        out_shape=(
            jax.ShapeDtypeStruct((16, 16, DP), BF),
            jax.ShapeDtypeStruct((16, 16, DP), BF),
            jax.ShapeDtypeStruct((2, 80, WA), BF),
            jax.ShapeDtypeStruct((2, 80, WB), BF),
        ),
        in_specs=[any_space] * 5,
        out_specs=(vmem,) * 4,
        scratch_shapes=scratch,
        compiler_params=pltpu.CompilerParams(
            collective_id=0, has_side_effects=True, vmem_limit_bytes=62 * 1024 * 1024
        ),
        name="layer",
    )(xc, wa, wb, jnp.asarray(cos), jnp.asarray(sin))

    ga = ga[:, :72].astype(F32)
    gb = gb[:, :72].astype(F32)
    g_q = jnp.concatenate([ga[0], ga[1, :, :64]], axis=1)
    g_kv = ga[1, :, 128:512].reshape(72, 3, 2, 64).transpose(0, 2, 1, 3).reshape(72, 384)
    g_out = jnp.concatenate([gb[0, :, 2304:2816], gb[1, :, 2304:2368]], axis=1).T
    g_down = jnp.concatenate([gb[0, :, 1536:2304], gb[1, :, 1536:2304]], axis=1).T
    return (
        by_token(bo),
        by_token(ig).astype(F32),
        ga[1, :, 64],
        g_q,
        g_kv,
        g_out,
        ga[1, :, 65],
        gb[0, :, :1536],
        gb[1, :, :1536],
        g_down,
    )


def solution(mesh):
    rows, model, last = P("fsdp", "ctx", None), P("fsdp", None), P(None, "fsdp")
    gain = P("fsdp")
    return jax.shard_map(
        local,
        mesh=mesh,
        in_specs=(rows, P("fsdp", "ctx"), gain, model, model, last, gain, model, model, last, rows),
        out_specs=(rows, rows, gain, model, model, last, gain, model, model, last),
        check_vma=False,
    )
```

time: 1040 us -> 214 us (0.21)
  waiting for transfers between devices: 575 us -> 0 us
  blocking collectives: 200 us -> 0 us
  Pallas kernels: 0 us -> 189 us
  matrix products: 97.9 us -> 0 us
  other arithmetic: 65.5 us -> 6.98 us
  local copies, waits for them, and re-layouts: 58.9 us -> 13.5 us
  between operations: 16 us -> 0.96 us
  loops' own time: 12.1 us -> 0 us
    reduce_scatter x4 -> x0, waiting for transfers between devices: 291 us -> none  [the longest x1 78.5 us: local(): lax.psum_scatter(grad_down.astype(jnp.bfloat16), 'fsdp', scatter_dimensio...]
    pallas_call x0 -> x1, Pallas kernels: none -> 189 us  [local(): pl.pallas_call(kernel, out_shape=(jax.ShapeDtypeStruct((16, 16, DP), BF),...]
    all_gather x4 -> x0, blocking collectives: 119 us -> none  [the longest x1 32.4 us: local(): lax.all_gather(w_query, 'fsdp', axis=0, tiled=True)]
    unnamed x15 -> x0, waiting for transfers between devices: 115 us -> none
    psum x1 -> x0, waiting for transfers between devices: 113 us -> none  [local(): lax.psum(shards[1].astype(jnp.bfloat16), 'ctx').astype(jnp.float32)]
    dot_general x130 -> x0, matrix products: 97.9 us -> none  [the longest x16 13.8 us: inner(): jnp.einsum('tgrd,kgd->tgrk', grad_att, value_rows, preferred_element_type...]
    all_gather x4 -> x0, waiting for transfers between devices: 56.7 us -> none  [the longest x1 50 us: local(): lax.all_gather(w_down, 'fsdp', axis=1, tiled=True)]
    psum x1 -> x0, blocking collectives: 49.8 us -> none  [local(): lax.psum(shards[0].astype(jnp.bfloat16), 'ctx').astype(jnp.float32)]
  transfers between devices with their start and end apart: 12 -> 0, of which waited for: 9 -> 0; matrix products, arithmetic and copies ran while one was open for 19% -> 0% of each run, Pallas kernels for 0% -> 0%
where the time goes in v1:
time: 214 us; the launch traced here: 210 us
  Pallas kernels  189 us (88%)
  local copies, waits for them, and re-layouts  13.5 us (6%)
  other arithmetic  6.98 us (3%)
    pallas_call x1, Pallas kernels, local(): pl.pallas_call(kernel, out_shape=(jax.ShapeDtypeStruct((16, 16, DP), BF),...  189 us

profile of v1, /device:TPU:23, one launch (start us, length us, event | category | flops | bytes accessed | tf_op | source)
XLA Modules:
  0.0 210.3 jit_solution(1395057214547151489)
XLA Ops:
  0.7 1.0 fusion.12
  1.7 0.7 slice.88
  2.4 1.1 concatenate.24
  3.5 0.9 slice.86
  4.4 1.0 fusion.2.wb_in
  5.9 0.4 reshape.125
  6.8 0.4 reshape_reshape.3
  7.3 0.5 broadcast.95
  7.8 0.7 reduce.7
  8.7 0.9 pad_maximum_fusion.xc
  10.4 0.7 fusion.5.wa_in
  11.1 188.8 %layer.1 = (bf16[16,16,640]{2,1,0:T(8,128)(2,1)}, bf16[16,16,640]{2,1,0:T(8,128)(2,1)}, bf16[2,80,512]{2,1,0:T(8,128)(2,1)}, bf16[2,80,2816]{2,1,0:T(8,128)(2,1)}) custom-call(bf16[16,32,640]{2,1,0:T(8,128)(2,1)} %pad_maximum_fusion.xc, bf16[2,80,512]{2,1,0:T(8,128)(2,1)} %fusion.5.wa_in, bf16[2,80,2816]{2,1,0:T(8,128)(2,1)} %fusion.2.wb_in, ...), custom_call_target="tpu_custom_call" | custom-call | tf_op jit(solution)/shard_map/layer/pallas_call | solution.py:652
  199.9 1.3 slice_convert_fusion
  201.2 0.8 maximum_bitcast_fusion
  202.1 0.7 maximum_bitcast_fusion.2
  202.8 0.7 pad_maximum_fusion.1
  203.5 1.0 slice_bitcast_fusion
  204.5 0.7 slice_reduce_fusion
  205.6 0.8 copy.43
  206.3 0.6 reshape.132
  207.4 1.0 copy.42
  208.4 0.6 reshape.130
  209.0 0.4 reshape.131
  209.4 0.9 copy.41
  (52 shorter events, 2.9 us)
Async XLA Ops:
  0.6 3.8 %copy-start.5 = (bf16[72,1536]{1,0:T(8,128)(2,1)S(1)}, bf16[72,1536]{1,0:T(8,128)(2,1)}, u32[]{:S(2)}) copy-start(bf16[72,1536]{1,0:T(8,128)(2,1)} %param.20) | copy-start | bytes 663556
  2.4 3.0 %copy-start.3 = (bf16[1,256,576]{1,2,0:T(8,128)(2,1)S(1)}, bf16[1,256,576]{1,2,0:T(8,128)(2,1)}, u32[]{:S(2)}) copy-start(bf16[1,256,576]{1,2,0:T(8,128)(2,1)} %param.13) | copy-start | bytes 884740
  5.4 1.0 copy-start.4
  5.9 1.9 copy-start.8
  6.8 2.8 %copy-start.7 = (bf16[72,384]{1,0:T(8,128)(2,1)S(1)}, bf16[72,384]{1,0:T(8,128)(2,1)}, u32[]{:S(2)}) copy-start(bf16[72,384]{1,0:T(8,128)(2,1)} %param.17) | copy-start | bytes 165892
  7.2 2.8 %copy-start.9 = (bf16[72]{0:T(256)(128)(2,1)S(1)}, bf16[72]{0:T(256)(128)(2,1)}, u32[]{:S(2)}) copy-start(bf16[72]{0:T(256)(128)(2,1)} %param.15) | copy-start | bytes 436
  7.3 2.9 %copy-start.10 = (bf16[72]{0:T(256)(128)(2,1)S(1)}, bf16[72]{0:T(256)(128)(2,1)}, u32[]{:S(2)}) copy-start(bf16[72]{0:T(256)(128)(2,1)} %param.19) | copy-start | bytes 436
  8.5 1.8 copy-start.2
  201.2 1.6 copy-start.6
  203.5 2.8 %copy-start.1 = (bf16[16,16,640]{2,1,0:T(8,128)(2,1)S(1)}, bf16[16,16,640]{2,1,0:T(8,128)(2,1)}, u32[]{:S(2)}) copy-start(bf16[16,16,640]{2,1,0:T(8,128)(2,1)} %get-tuple-element.15) | copy-start | bytes 983044
  207.0 1.4 copy-start

commit v2 on v1

--- a/solution.py
+++ b/solution.py
@@ -14,11 +14,13 @@
 DP = 640
 ROWS = 256
 WA = 512
-WB = 2816
+TB = 24
 FC = 256
 NEG = -1e30
 STEPS = (0, 1, 3, 2)
 BACK = (2, 1, 3, 0)
+LAST = (1, 2)
+CHIPS = ((0, 1), (0, 3), (1, 0), (1, 1), (1, 3), (0, 2), (1, 2))
 
 
 def mm(a, b):
@@ -31,6 +33,14 @@
 
 def mm_tn(a, b):
     return lax.dot_general(a, b, (((0,), (0,)), ((), ())), preferred_element_type=F32)
+
+
+def up_tile(half, t):
+    return t if t < 10 else t + (6 if half == 0 else 4)
+
+
+def down_tile(t):
+    return t // 6, 10 + t % 6 if t < 10 else 6 + t
 
 
 def lane_iota(shape):
@@ -43,14 +53,16 @@
 
 
 def kernel(
-    xc, wa_in, wb_in, cos_in, sin_in,
+    pos, g1_in, g2_in, tok_h, cot_h, wq_h, wkv_h, wo_h, wg_h, wu_h, wd_h, cols_h, rows_h, cos_in, sin_in,
     bo_out, ig_out, ga_out, gb_out,
-    xc_r, wa, wb, cos_s, sin_s, kv, bias, perm,
+    tok, cot, wq_in, wkv_in, wo_in, wg_in, wu_in, wd_in, spread_cols, spread_rows,
+    xc, wa_in, wb_in, xc_r, wa, wb, cos_s, sin_s, kv, bias, perm,
     qt, qx, dot_, dox, st_m, st_l, acc, ot, dqt,
     xs, dy, mid, act1, act1t, attb, dmid,
-    dkv_p, d1_r, d2_s, d2_r,
-    ga, gac, gbc, gax, gbx, ga2, gb2, gaz, gbz, ga3, gb3, gal, gbl, ga4, gb4, gay, gby,
-    gaf, gbf, bo_s, bo_r, ig_s, ig_r,
+    dkv_p, d1_r, d2_s, d2_r, dz_s, dz_r,
+    ga, gac, gax, gay_s, gay, gaf,
+    gbc, q1, t1, q2, t2, q3, gbf,
+    bo_s, bo_r, ig_s, ig_r,
     ss, rs, ls,
 ):
     f = lax.axis_index("fsdp")
@@ -88,18 +100,112 @@
     def arrived(dst, sem):
         remote(dst, dst, sem, f, other).wait_recv()
 
+    loads = [
+        pltpu.make_async_copy(src, dst, ls.at[7 + n])
+        for n, (src, dst) in enumerate(
+            (
+                (wq_h, wq_in), (wkv_h, wkv_in), (tok_h, tok), (cols_h, spread_cols),
+                (rows_h, spread_rows), (cot_h, cot), (wg_h, wg_in), (wu_h, wu_in), (wd_h, wd_in),
+                (wo_h, wo_in),
+            )
+        )
+    ]
+    for copy in loads:
+        copy.start()
+
     barrier = pltpu.get_barrier_semaphore()
     for step in range(1, 16):
         pl.semaphore_signal(
             barrier, inc=1, device_id={"fsdp": f, "ctx": (c + step) % 16}, device_id_type=MESH
         )
-    pl.semaphore_signal(barrier, inc=1, device_id={"fsdp": fz, "ctx": c}, device_id_type=MESH)
-    for step in range(1, 4):
+    for step in range(1, 8):
         pl.semaphore_signal(
-            barrier, inc=1, device_id={"fsdp": zh * 4 + (xx + step) % 4, "ctx": c},
-            device_id_type=MESH,
+            barrier, inc=1, device_id={"fsdp": (f + step) % 8, "ctx": c}, device_id_type=MESH
         )
-    pl.semaphore_wait(barrier, 19)
+    pl.semaphore_signal(
+        barrier, inc=1, device_id={"fsdp": fz, "ctx": ctx_at(1 - zl, yy, k)}, device_id_type=MESH
+    )
+
+    rows_of = lax.broadcasted_iota(jnp.int32, (ROWS, 1), 0)
+    run = jnp.where((rows_of // 8) % 2 == 0, pos[0, 0], pos[0, 128]).astype(F32)
+    tag = run * (1.0 / 16.0) + (rows_of % 8).astype(F32)
+
+    def pack_rows(ref):
+        return mm(spread_rows[...], mm_tn(ref[...], spread_cols[...]).astype(BF))
+
+    for copy in loads:
+        copy.wait()
+    xc[:, 0:16, :] = (
+        jnp.where(lane_iota((ROWS, DP)) == 72, tag, pack_rows(tok)).astype(BF).reshape(16, 16, DP)
+    )
+    xc[:, 16:32, :] = pack_rows(cot).astype(BF).reshape(16, 16, DP)
+
+    def pad_rows(value):
+        return jnp.concatenate([value.astype(F32), jnp.zeros((8, value.shape[1]), F32)], axis=0)
+
+    wq_all = pad_rows(wq_in[...])
+    wkv_all = pad_rows(wkv_in[...])
+    low80 = lane_iota((80, 128)) < 64
+    wa_in[0] = wq_all[:, 0:512].astype(BF)
+    row16 = lax.broadcasted_iota(jnp.int32, (16, 72), 0)
+    gains_in = jnp.where(row16 == 0, g1_in[...].astype(F32), g2_in[...].astype(F32))
+    gains_in = jnp.where(row16 < 2, gains_in, 0.0).astype(BF)
+    row_hot = lax.broadcasted_iota(jnp.int32, (16, 128), 0)
+    gain_hot = jnp.where((lane_iota((16, 128)) == 64 + row_hot) & (row_hot < 2), 1.0, 0.0).astype(BF)
+    last_q = jnp.concatenate([wq_all[:, 512:576], jnp.zeros((80, 64), F32)], axis=1)
+    wa_in[1, :, 0:128] = (last_q + pad_rows(mm_tn(gains_in, gain_hot))).astype(BF)
+
+    def kv_head(n, want_low):
+        block = wkv_all[:, 128 * (n // 2) : 128 * (n // 2) + 128]
+        return block if (n % 2 == 0) == want_low else pltpu.roll(block, 64, 1)
+
+    for g in range(3):
+        both = jnp.where(low80, kv_head(g, True), kv_head(3 + g, False))
+        wa_in[1, :, 128 + 128 * g : 256 + 128 * g] = both.astype(BF)
+
+    for half, ref in ((0, wg_in), (1, wu_in)):
+        whole = pad_rows(ref[...]).astype(BF)
+        for t in range(12):
+            wb_in[half, up_tile(half, t)] = whole[:, 128 * t : 128 * t + 128]
+    whole = pad_rows(wd_in[...]).astype(BF)
+    for t in range(12):
+        half, at = down_tile(t)
+        wb_in[half, at] = whole[:, 128 * t : 128 * t + 128]
+    whole = jnp.concatenate([pad_rows(wo_in[...]), jnp.zeros((80, 64), F32)], axis=1).astype(BF)
+    for t in range(5):
+        wb_in[t // 4, 18 + t % 4] = whole[:, 128 * t : 128 * t + 128]
+    wb_in[0, 22:24] = jnp.zeros((2, 80, 128), BF)
+    wb_in[1, 19:24] = jnp.zeros((5, 80, 128), BF)
+    pl.semaphore_wait(barrier, 23)
+
+    zz = 2 * zh + zl
+    order = ("ayb", "yba", "yab")
+
+    def pick(n, u, w):
+        return u if n < 2 else u * (1 - k) + w * k
+
+    def coord(n, axis):
+        if axis == "y":
+            return yy
+        return pick(n, zz, xx) if axis == "a" else pick(n, xx, zz)
+
+    def along(n, axis, step):
+        if axis == "y":
+            return f, ctx_at(zl, (yy + step) % 4, k)
+        z = (zz + step) % 4
+        by_x = (zh * 4 + (xx + step) % 4, c)
+        by_z = ((z // 2) * 4 + xx, ctx_at(z % 2, yy, k))
+        first, second = (by_z, by_x) if axis == "a" else (by_x, by_z)
+        return pick(n, first[0], second[0]), pick(n, first[1], second[1])
+
+    def region(n, done, axis=None, step=0):
+        at = []
+        for name in "aby":
+            if name in done:
+                at.append(slice(None))
+            else:
+                at.append((coord(n, name) + 4 - step) % 4 if name == axis else coord(n, name))
+        return wb.at[(k, n, *at)]
 
     sem_x = take(16)
     for step in range(1, 16):
@@ -107,9 +213,14 @@
     local = [
         pltpu.make_async_copy(xc.at[c], xc_r.at[c], ls.at[0]),
         pltpu.make_async_copy(wa_in.at[k], wa.at[k, f], ls.at[1]),
-        pltpu.make_async_copy(wb_in.at[k], wb.at[k, f], ls.at[2]),
-        pltpu.make_async_copy(cos_in.at[:, c], cos_s, ls.at[3]),
-        pltpu.make_async_copy(sin_in.at[:, c], sin_s, ls.at[4]),
+        *(
+            pltpu.make_async_copy(
+                wb_in.at[k, 8 * n + 2 * yy + zl], region(n, ()), ls.at[4 + n]
+            )
+            for n in range(3)
+        ),
+        pltpu.make_async_copy(cos_in.at[:, c], cos_s, ls.at[2]),
+        pltpu.make_async_copy(sin_in.at[:, c], sin_s, ls.at[3]),
     ]
     for copy in local:
         copy.start()
@@ -136,10 +247,35 @@
     def gather_last(w, sem):
         arrived(w.at[1 - k], sem + 7)
 
+    sem_b = take(30)
+
+    def spread(turn):
+        if turn > 0:
+            spread_wait(turn - 1)
+        out = []
+        for n in range(3):
+            axis, done = order[n][turn], order[n][:turn]
+            for step in range(1, 4):
+                if turn == 0:
+                    src = wb_in.at[k, 8 * n + 2 * yy + zl]
+                else:
+                    src = region(n, done)
+                copy = send(
+                    src, region(n, done), sem_b + 9 * turn + 3 * n + step - 1, *along(n, axis, step)
+                )
+                if turn > 0:
+                    out.append(copy)
+        return out
+
+    def spread_wait(turn, groups=(0, 1, 2)):
+        for n in groups:
+            axis, done = order[n][turn], order[n][:turn]
+            for step in range(1, 4):
+                arrived(region(n, done, axis, step), sem_b + 9 * turn + 3 * n + step - 1)
+
     sem_a = take(8)
-    sem_b = take(8)
     gather_first(wa_in, wa, sem_a)
-    gather_first(wb_in, wb, sem_b)
+    spread(0)
 
     def make_bias(slot, carry):
         e = ctx_at((slot // 2) % 2, slot // 4, slot % 2)
@@ -167,6 +303,7 @@
     xs[...] = x
     dy[...] = mm(perm_t, xc_r[:, 16:32, :].reshape(ROWS, DP)).astype(BF)
 
+    from_wb = spread(1)
     gather_third(wa, sem_a)
     r1 = lax.rsqrt(jnp.sum(x * x, axis=-1, keepdims=True) * (1.0 / D) + 1e-5)
     gather_last(wa, sem_a)
@@ -195,12 +332,15 @@
         kv[mine, g] = (u * cos_kv + partner_lanes(u) * sin_kv).astype(BF)
     sem_k = take(16)
 
+    near = slot_at(1 - zl, yy, k)
+
+    def kv_along_y(slot, a):
+        for off in STEPS[1:]:
+            send(kv.at[slot], kv.at[slot], sem_k + a * 4 + off, f, ctx_at(zl, (yy + off) % 4, k))
+
     send(kv.at[mine], kv.at[mine], sem_k, f, other)
-    for off in STEPS:
-        for a in (0, 1):
-            if (a, off) != (0, 0):
-                to = ctx_at(zl if a == 0 else 1 - zl, (yy + off) % 4, k)
-                send(kv.at[mine], kv.at[mine], sem_k + a * 4 + off, f, to)
+    send(kv.at[mine], kv.at[mine], sem_k + 4, f, ctx_at(1 - zl, yy, k))
+    kv_along_y(mine, 0)
 
     def kv_direct(off):
         for a in (0, 1):
@@ -213,6 +353,8 @@
         for a in (0, 1):
             at = slot_at(zl if a == 0 else 1 - zl, (yy + 4 - off) % 4, 1 - k)
             arrived(kv.at[at], sem_k if (a, off) == (0, 0) else sem_k + 8 + a * 4 + off)
+
+    from_wb += spread(2)
 
     for t in range(5):
         w = wa[0, :, :, 128 * t : 128 * t + 128] if t < 4 else wa[1, :, :, 0:128]
@@ -229,7 +371,8 @@
                     qx[g, at : at + 128, :] = v[128 * ih : 128 * ih + 128].astype(BF)
                     qt[g, :, at : at + 128] = vt[:, 128 * ih : 128 * ih + 128].astype(BF)
 
-    from_wb = gather_second(wb, sem_b)
+    kv_direct(0)
+    kv_along_y(near, 1)
 
     st_m[...] = jnp.full(st_m.shape, NEG, F32)
     st_l[...] = jnp.zeros(st_l.shape, F32)
@@ -265,7 +408,6 @@
 
         lax.fori_loop(0, 3, per_head, 0)
 
-    kv_direct(0)
     kv_direct(STEPS[1])
     kv_across(0)
     fold_forward(0)
@@ -275,8 +417,10 @@
     kv_direct(STEPS[3])
     kv_across(STEPS[2])
     fold_forward(STEPS[2])
-    from_wb += gather_third(wb, sem_b)
     kv_across(STEPS[3])
+    for n in (1, 0, 2):
+        spread_wait(2, (n,))
+        from_wb.append(send(wb.at[k, n], wb.at[k, n], sem_b + 27 + n, f, other))
     fold_forward(STEPS[3])
 
     def head_rows(ref, g, r):
@@ -292,14 +436,39 @@
         b = head_rows(ot, (2 * t + 1) // 3, (2 * t + 1) % 3) if t < 4 else jnp.zeros((ROWS, 128), F32)
         attb[:, 128 * t : 128 * t + 128] = jnp.where(low, a, b).astype(BF)
 
-    gather_last(wb, sem_b)
-
-    def out_t(half):
-        if half == 0:
-            return wb[0, :, :, 2304:2816].reshape(DP, 512)
-        return wb[1, :, :, 2304:2432].reshape(DP, 128)
-
-    m0 = xs[...] + mm_nt(attb[:, 0:512], out_t(0)) + mm_nt(attb[:, 512:640], out_t(1))
+    for n in range(3):
+        arrived(wb.at[1 - k, n], sem_b + 27 + n)
+
+    def fixed(half, n):
+        return isinstance(half, int) and isinstance(n, int) and (half, n) == LAST
+
+    def tile_at(half, n, y, z):
+        if fixed(half, n):
+            blocks = [wb[1, 2, :, 2 * q + z, y] for q in range(2)]
+        else:
+            blocks = [wb[half, n, 2 * q + z, :, y] for q in range(2)]
+        return jnp.concatenate(blocks, axis=0).reshape(DP, 128)
+
+    def put_tile(half, n, y, z, value):
+        value = value.astype(BF).reshape(2, 4, 80, 128)
+        for q in range(2):
+            if fixed(half, n):
+                wb[1, 2, :, 2 * q + z, y] = value[q]
+            else:
+                wb[half, n, 2 * q + z, :, y] = value[q]
+
+    def pair(half, p):
+        return jnp.concatenate([tile_at(half, p // 4, p % 4, z) for z in range(2)], axis=1)
+
+    def put_pair(half, p, value):
+        for z in range(2):
+            put_tile(half, p // 4, p % 4, z, value[:, 128 * z : 128 * z + 128])
+
+    def out_tile(t):
+        return tile_at(0, 2, 1 + t // 2, t % 2) if t < 4 else tile_at(1, 2, 1, 0)
+
+    out_w = jnp.concatenate([out_tile(t) for t in range(5)], axis=1)
+    m0 = xs[...] + mm_nt(attb[...], out_w)
     r2 = lax.rsqrt(jnp.sum(m0 * m0, axis=-1, keepdims=True) * (1.0 / D) + 1e-5)
     mid[...] = m0
     a2 = m0 * r2 * gain2
@@ -311,15 +480,12 @@
     for copy in from_wb:
         copy.wait_send()
     sends[:] = [copy for copy in sends if all(copy is not done for done in from_wb)]
-    gb = wb
 
     def ff(j, carry):
         total, dact = carry
-        cols = pl.ds(pl.multiple_of(j * FC, FC), FC)
-        dcol = pl.ds(pl.multiple_of(1536 + (j % 3) * FC, FC), FC)
-        wg = wb[0, :, :, cols].reshape(DP, FC)
-        wu = wb[1, :, :, cols].reshape(DP, FC)
-        wd = wb[j // 3, :, :, dcol].reshape(DP, FC)
+        last = isinstance(j, int)
+        at_g, at_u, at_d = ((0, 8), (1, 7), (1, 8)) if last else ((0, j), (1, j), (j // 3, 5 + j % 3))
+        wg, wu, wd = pair(*at_g), pair(*at_u), pair(*at_d)
         gate, up = mm(a2b, wg), mm(a2b, wu)
         sig = jax.nn.sigmoid(gate)
         swish = gate * sig
@@ -328,14 +494,132 @@
         dh = mm(dyb, wd)
         dg = (dh * up * sig * (1.0 + gate * (1.0 - sig))).astype(BF)
         du = (dh * swish).astype(BF)
-        gb[j // 3, :, :, dcol] = mm(dyt, hid).astype(BF).reshape(8, 80, FC)
-        gb[0, :, :, cols] = mm(a2t, dg).astype(BF).reshape(8, 80, FC)
-        gb[1, :, :, cols] = mm(a2t, du).astype(BF).reshape(8, 80, FC)
+        put_pair(*at_d, mm(dyt, hid))
+        put_pair(*at_g, mm(a2t, dg))
+        put_pair(*at_u, mm(a2t, du))
         dact = dact + mm_nt(dg, wg) + mm_nt(du, wu)
         return total, dact
 
     zero = jnp.zeros((ROWS, DP), F32)
-    total, dact = lax.fori_loop(0, 6, ff, (zero, zero))
+    total, dact = ff(5, lax.fori_loop(0, 5, ff, (zero, zero)))
+
+    sem_r = take(42)
+
+    def add(ref, at, got_at):
+        v = ref[at].astype(F32)
+        for r in got_at:
+            v = v + r.astype(F32)
+        return v
+
+    def red_core(n):
+        send(wb.at[1 - k, n], gbc.at[n], sem_r + n, f, other)
+
+    def red_one(n):
+        arrived(gbc.at[n], sem_r + n)
+
+        def body(i, carry):
+            wb[k, n, i // 4, i % 4] = (
+                wb[k, n, i // 4, i % 4].astype(F32) + gbc[n, i // 4, i % 4].astype(F32)
+            ).astype(BF)
+            return carry
+
+        lax.fori_loop(0, 16, body, 0)
+        axis = order[n][2]
+        for step in range(1, 4):
+            to = (coord(n, axis) + step) % 4
+            src = wb.at[k, n, to] if axis == "a" else wb.at[k, n, :, to]
+            send(src, q1.at[n, step - 1], sem_r + 3 + 3 * n + step - 1, *along(n, axis, step))
+
+    def red_two(n):
+        for step in range(3):
+            arrived(q1.at[n, step], sem_r + 3 + 3 * n + step)
+        axis, at = order[n][2], coord(n, order[n][2])
+
+        def body(i, carry):
+            v = (wb[k, n, at, i] if axis == "a" else wb[k, n, i, at]).astype(F32)
+            for step in range(3):
+                v = v + q1[n, step, i].astype(F32)
+            t1[n, i] = v.astype(BF)
+            return carry
+
+        lax.fori_loop(0, 4, body, 0)
+        axis = order[n][1]
+        for step in range(1, 4):
+            to = (coord(n, axis) + step) % 4
+            src = t1.at[n, :, to] if axis == "y" else t1.at[n, to]
+            send(src, q2.at[n, step - 1], sem_r + 12 + 3 * n + step - 1, *along(n, axis, step))
+
+    def red_three(n):
+        for step in range(3):
+            arrived(q2.at[n, step], sem_r + 12 + 3 * n + step)
+        axis, at = order[n][1], coord(n, order[n][1])
+        own = (n, slice(None), at) if axis == "y" else (n, at)
+        t2[n] = add(t1, own, [q2[n, i] for i in range(3)]).astype(BF)
+        axis = order[n][0]
+        for step in range(1, 4):
+            to = (coord(n, axis) + step) % 4
+            send(t2.at[n, to], q3.at[n, step - 1], sem_r + 21 + 3 * n + step - 1, *along(n, axis, step))
+
+    def red_four():
+        for n in range(3):
+            for step in range(3):
+                arrived(q3.at[n, step], sem_r + 21 + 3 * n + step)
+            own = add(t2, (n, coord(n, order[n][0])), [q3[n, i] for i in range(3)])
+            gbf[k, yy, zl, n] = own.astype(BF)
+        piece = gbf.at[k, yy, zl]
+        for a, off in CHIPS:
+            to = ctx_at(zl if a == 0 else 1 - zl, (yy + off) % 4, k)
+            send(piece, piece, sem_r + 30 + 4 * a + off, f, to)
+
+    def red_five():
+        for a, off in CHIPS:
+            z = zl if a == 0 else 1 - zl
+            arrived(gbf.at[k, (yy + 4 - off) % 4, z], sem_r + 30 + 4 * a + off)
+        send(gbf.at[k], gbf.at[k], sem_r + 38, f, other)
+
+    def red_six():
+        arrived(gbf.at[1 - k], sem_r + 38)
+
+    sem_g = take(24)
+
+    def in_core():
+        send(ga.at[1 - k], gac, sem_g, f, other)
+
+    def in_one():
+        arrived(gac, sem_g)
+        ga[k] = (ga[k].astype(F32) + gac[...].astype(F32)).astype(BF)
+        for step in range(1, 8):
+            to = (f + step) % 8
+            send(ga.at[k, to], gax.at[step - 1], sem_g + step, to, c)
+
+    def in_two():
+        for step in range(1, 8):
+            arrived(gax.at[step - 1], sem_g + step)
+        v = add(ga, (k, f), [gax[i] for i in range(7)])
+        for t in range(4):
+            gay_s[t] = v[:, 128 * t : 128 * t + 128].astype(BF)
+        for a, off in CHIPS:
+            y = (yy + off) % 4
+            to = ctx_at(zl if a == 0 else 1 - zl, y, k)
+            send(gay_s.at[y], gay.at[4 * a + off], sem_g + 8 + 4 * a + off, f, to)
+
+    def in_three():
+        for a, off in CHIPS:
+            arrived(gay.at[4 * a + off], sem_g + 8 + 4 * a + off)
+        gaf[k, yy] = add(gay_s, yy, [gay[4 * a + off] for a, off in CHIPS]).astype(BF)
+        for step in range(1, 4):
+            send(gaf.at[k, yy], gaf.at[k, yy], sem_g + 16 + step, *along(0, "y", step))
+
+    def in_four():
+        for step in range(1, 4):
+            arrived(gaf.at[k, (yy + 4 - step) % 4], sem_g + 16 + step)
+        send(gaf.at[k], gaf.at[k], sem_g + 20, f, other)
+
+    def in_five():
+        arrived(gaf.at[1 - k], sem_g + 20)
+
+    red_core(0)
+    red_core(1)
 
     def give_back(value, src, dst, sem):
         src[...] = mm(perm[...], value.astype(BF)).astype(BF).reshape(16, 16, DP)
@@ -357,73 +641,8 @@
     dmb = dm.astype(BF)
     dmt = dm.T.astype(BF)
 
-    def reducer(width, parts, core_r, x_r, sum2, z_r, sum3, l_r, sum4, y_r, final):
-        sem = take(9)
-        half = width // 2
-        mine_cols = pl.ds(pl.multiple_of(zl * half, 128), half)
-        their_cols = pl.ds(pl.multiple_of((1 - zl) * half, 128), half)
-
-        def one():
-            send(parts.at[1 - k], core_r, sem, f, other)
-
-        def two():
-            arrived(core_r, sem)
-            parts[k] = (parts[k].astype(F32) + core_r[...].astype(F32)).astype(BF)
-            for step in range(1, 4):
-                to = (xx + step) % 4
-                for q in range(2):
-                    pair = x_r.at[step - 1, q]
-                    send(parts.at[k, q * 4 + to], pair, sem_x2 + 2 * (step - 1) + q, q_f(to), c)
-
-        def three_():
-            for step in range(3):
-                for q in range(2):
-                    arrived(x_r.at[step, q], sem_x2 + 2 * step + q)
-            for q in range(2):
-                v = parts[k, q * 4 + xx].astype(F32)
-                for step in range(3):
-                    v = v + x_r[step, q].astype(F32)
-                sum2[q] = v.astype(BF)
-            send(sum2.at[1 - zh], z_r, sem + 1, fz, c)
-
-        def four():
-            arrived(z_r, sem + 1)
-            sum3[...] = (sum2[zh].astype(F32) + z_r[...].astype(F32)).astype(BF)
-            send(sum3.at[:, their_cols], l_r, sem + 2, f, ctx_at(1 - zl, yy, k))
-
-        def five():
-            arrived(l_r, sem + 2)
-            sum4[...] = (sum3[:, mine_cols].astype(F32) + l_r[...].astype(F32)).astype(BF)
-            for step in range(1, 4):
-                send(sum4, y_r.at[step - 1], sem + 2 + step, f, ctx_at(zl, (yy + step) % 4, k))
-
-        def six():
-            for step in range(1, 4):
-                arrived(y_r.at[step - 1], sem + 2 + step)
-            v = sum4[...].astype(F32)
-            for step in range(3):
-                v = v + y_r[step].astype(F32)
-            final[k, :, mine_cols] = v.astype(BF)
-            piece = final.at[k, :, mine_cols]
-            send(piece, piece, sem + 6, f, ctx_at(1 - zl, yy, k))
-
-        def seven():
-            arrived(final.at[k, :, their_cols], sem + 6)
-            send(final.at[k], final.at[k], sem + 7, f, other)
-
-        def eight():
-            arrived(final.at[1 - k], sem + 7)
-
-        sem_x2 = take(6)
-
-        def q_f(to):
-            return zh * 4 + to
-
-        return one, two, three_, four, five, six, seven, eight
-
     for t in range(5):
-        w = wb[0, :, :, 2304 + 128 * t : 2432 + 128 * t] if t < 4 else wb[1, :, :, 2304:2432]
-        u = mm(dmb, w.reshape(DP, 128)).astype(BF).astype(F32)
+        u = mm(dmb, out_tile(t)).astype(BF).astype(F32)
         for half in range(2):
             h = 2 * t + half
             if h < 9:
@@ -434,10 +653,12 @@
                     at = 384 * ih + 128 * r
                     dox[g, at : at + 128, :] = v[128 * ih : 128 * ih + 128].astype(BF)
                     dot_[g, :, at : at + 128] = vt[:, 128 * ih : 128 * ih + 128].astype(BF)
-    gb[0, :, :, 2304:2816] = mm(dmt, attb[:, 0:512]).astype(BF).reshape(8, 80, 512)
-    gb[1, :, :, 2304:2432] = mm(dmt, attb[:, 512:640]).astype(BF).reshape(8, 80, 128)
-    red_b = reducer(WB, gb, gbc, gbx, gb2, gbz, gb3, gbl, gb4, gby, gbf)
-    red_b[0]()
+    grad_out = mm(dmt, attb[...]).astype(BF)
+    for t in range(5):
+        at = (0, 2, 1 + t // 2, t % 2) if t < 4 else (1, 2, 1, 0)
+        put_tile(*at, grad_out[:, 128 * t : 128 * t + 128])
+    red_core(2)
+
     for g in range(3):
         st_m[g] = jnp.sum(dot_[g].astype(F32) * ot[g], axis=0, keepdims=True)
     dqt[...] = jnp.zeros(dqt.shape, F32)
@@ -471,7 +692,8 @@
 
         lax.fori_loop(0, 3, per_head, 0)
 
-    sem_d = take(12)
+    sem_d1 = take(8)
+    sem_d = take(4)
 
     def dkv_first(at_step):
         for z in range(2):
@@ -479,8 +701,6 @@
                 dkv_p.at[at_step, 2 * z + 1 - k], d1_r.at[at_step, z], sem_d1 + 2 * at_step + z,
                 f, other,
             )
-
-    sem_d1 = take(8)
 
     def dkv_second(at_step, off):
         for z in range(2):
@@ -489,28 +709,30 @@
             d2_s[at_step, z] = (
                 dkv_p[at_step, 2 * z + k].astype(F32) + d1_r[at_step, z].astype(F32)
             ).astype(BF)
-        for a in (0, 1):
-            if (a, off) != (0, 0):
-                z = zl if a == 0 else 1 - zl
-                send(
-                    d2_s.at[at_step, z], d2_r.at[a * 4 + off], sem_d + a * 4 + off,
-                    f, ctx_at(z, (yy + 4 - off) % 4, k),
-                )
-
+        if off != 0:
+            send(
+                d2_s.at[at_step], d2_r.at[off - 1], sem_d + off,
+                f, ctx_at(zl, (yy + 4 - off) % 4, k),
+            )
+
+    red_one(0)
+    red_one(1)
+    red_one(2)
     fold_backward(0, BACK[0])
     dkv_first(0)
-    red_b[1]()
+    dkv_second(0, BACK[0])
     fold_backward(1, BACK[1])
     dkv_first(1)
-    dkv_second(0, BACK[0])
+    dkv_second(1, BACK[1])
     fold_backward(2, BACK[2])
     dkv_first(2)
-    dkv_second(1, BACK[1])
-    red_b[2]()
+    dkv_second(2, BACK[2])
+    for n in range(3):
+        red_two(n)
     fold_backward(3, BACK[3])
     dkv_first(3)
-    dkv_second(2, BACK[2])
-    red_b[3]()
+    for n in range(3):
+        red_three(n)
 
     dq_tiles = []
     for t in range(5):
@@ -527,17 +749,17 @@
     dact1 = mm_nt(dq[:, 0:512], wa[0].reshape(DP, 512)) + mm_nt(
         dq[:, 512:640], wa[1, :, :, 0:128].reshape(DP, 128)
     )
-    red_b[4]()
     dkv_second(3, BACK[3])
-
-    for a in (0, 1):
-        for off in range(4):
-            if (a, off) != (0, 0):
-                arrived(d2_r.at[a * 4 + off], sem_d + a * 4 + off)
+    for off in range(1, 4):
+        arrived(d2_r.at[off - 1], sem_d + off)
+    dz_s[...] = add(d2_s, (3, 1 - zl), [d2_r[i, 1 - zl] for i in range(3)]).astype(BF)
+    send(dz_s, dz_r, sem_d, f, ctx_at(1 - zl, yy, k))
+    red_four()
+    dkv = add(d2_s, (3, zl), [d2_r[i, zl] for i in range(3)])
+    arrived(dz_r, sem_d)
+    dkv = dkv + dz_r[...].astype(F32)
     for g in range(3):
-        u = d2_s[3, zl, g].astype(F32)
-        for n in range(1, 8):
-            u = u + d2_r[n, g].astype(F32)
+        u = dkv[g]
         u = (u * cos_kv - partner_lanes(u) * sin_kv).astype(BF)
         at = 128 + 128 * g
         ga[1, :, :, at : at + 128] = mm(a1t, u).astype(BF).reshape(8, 80, 128)
@@ -552,31 +774,27 @@
     hot = jnp.where(lax.broadcasted_iota(jnp.int32, (8, 128), 0) < 2, hot, 0.0)
     gain_cols = mm(gains.T.astype(BF), hot.astype(BF))
     ga[1, :, :, 0:128] = (mm(a1t, dq[:, 512:640]) + gain_cols).astype(BF).reshape(8, 80, 128)
-    red_a = reducer(WA, ga, gac, gax, ga2, gaz, ga3, gal, ga4, gay, gaf)
-    red_a[0]()
+    in_core()
 
     wgt = dact1 * gain1
     inner = jnp.sum(wgt * x, axis=-1, keepdims=True) * (1.0 / D)
     give_back(
         dmid[...] + r1 * wgt - x * (r1 * r1 * r1) * inner, ig_s, ig_r, sem_i
     )
-    red_a[1]()
-    red_b[5]()
-    red_a[2]()
-    red_b[6]()
-    red_a[3]()
-    red_a[4]()
-    red_b[7]()
-    gb_out[...] = gbf[...]
-    red_a[5]()
+    in_one()
+    red_five()
     for step in range(1, 16):
         arrived(bo_r.at[(c + 16 - step) % 16], sem_o + step)
     bo_out[...] = bo_r[...]
-    red_a[6]()
+    red_six()
+    gb_out[...] = gbf[...]
+    in_two()
+    in_three()
     for step in range(1, 16):
         arrived(ig_r.at[(c + 16 - step) % 16], sem_i + step)
     ig_out[...] = ig_r[...]
-    red_a[7]()
+    in_four()
+    in_five()
     ga_out[...] = gaf[...]
     for copy in sends:
         copy.wait_send()
@@ -592,37 +810,74 @@
     return cos.reshape(shape).astype(np.float32), sin.reshape(shape).astype(np.float32)
 
 
-def pad_model(rows):
-    return jnp.pad(rows.reshape(ROWS, 8, 72), ((0, 0), (0, 0), (0, 8))).reshape(ROWS, DP)
-
-
-def by_target(rows):
-    return rows.reshape(2, 16, 8, DP).transpose(1, 0, 2, 3).reshape(16, 16, DP)
-
-
-def by_token(rows):
-    rows = rows.reshape(16, 2, 8, 8, 80)[..., :72]
-    return rows.transpose(1, 0, 2, 3, 4).reshape(1, ROWS, D)
+def placements():
+    cols = np.zeros((D, DP), np.float32)
+    at = np.arange(D)
+    cols[at, at // 72 * 80 + at % 72] = 1.0
+    rows = np.zeros((ROWS, ROWS), np.float32)
+    at = np.arange(ROWS)
+    rows[at, at // 8 % 2 * 128 + at // 16 * 8 + at % 8] = 1.0
+    return jnp.asarray(cols, BF), jnp.asarray(rows, BF)
+
+
+def finish(
+    bo_h, ig_h, ga_h, gb_h, cols_h, rows_h,
+    out, grad_in, n1, gq, gkv, go, n2, gg, gu, gd,
+    bo, ig, ga, gb, cols, rows, sems,
+):
+    copies = [
+        pltpu.make_async_copy(src, dst, sems.at[n])
+        for n, (src, dst) in enumerate(
+            ((gb_h, gb), (cols_h, cols), (rows_h, rows), (bo_h, bo), (ig_h, ig), (ga_h, ga))
+        )
+    ]
+    for copy in copies:
+        copy.start()
+    for copy in copies:
+        copy.wait()
+    for src, dst in ((bo, out), (ig, grad_in)):
+        narrow = mm_nt(cols[...], src[...].reshape(ROWS, DP)).astype(BF)
+        dst[...] = mm(narrow, rows[...]).astype(dst.dtype)
+
+    def part(ref, *at):
+        return ref[at].astype(F32)
+
+    for t in range(4):
+        gq[:, 128 * t : 128 * t + 128] = part(ga, 0, t)[0:72]
+    last = part(ga, 1, 0)
+    gq[:, 512:576] = last[0:72, 0:64]
+    row = lax.broadcasted_iota(jnp.int32, (16, 128), 0)
+    hot = jnp.where((lane_iota((16, 128)) == 64 + row) & (row < 2), 1.0, 0.0).astype(BF)
+    gains = mm_nt(hot, ga[1, 0])
+    n1[...] = gains[0:1, 0:72]
+    n2[...] = gains[1:2, 0:72]
+    low = lane_iota((80, 128)) < 64
+    tiles = [part(ga, 1, 1 + g) for g in range(3)]
+    turn = [pltpu.roll(t, 64, 1) for t in tiles]
+    heads = [
+        jnp.where(low, tiles[0], turn[1]),
+        jnp.where(low, tiles[2], tiles[0]),
+        jnp.where(low, turn[1], tiles[2]),
+    ]
+    for g in range(3):
+        gkv[:, 128 * g : 128 * g + 128] = heads[g][0:72]
+
+    def tile(half, t):
+        return part(gb, half, (t % 8) // 2, t % 2, t // 8)
+
+    for half, ref in ((0, gg), (1, gu)):
+        for t in range(12):
+            ref[:, 128 * t : 128 * t + 128] = tile(half, up_tile(half, t))[0:72]
+    for t in range(12):
+        gd[:, 128 * t : 128 * t + 128] = tile(*down_tile(t))[0:72]
+    for t in range(4):
+        go[:, 128 * t : 128 * t + 128] = tile(0, 18 + t)[0:72]
+    go[:, 512:576] = tile(1, 18)[0:72, 0:64]
 
 
 def local(tokens, positions, gain1, wq, wkv, wo, gain2, wg, wu, wd, cotangent):
-    place = (positions[0] // 128) * 8 + positions[0] % 8
-    x = pad_model(tokens[0])
-    x = jnp.where(lane_iota((ROWS, DP)) == 72, place[:, None].astype(BF), x)
-    xc = jnp.concatenate([by_target(x), by_target(pad_model(cotangent[0]))], axis=1)
-    w_kv = wkv.reshape(72, 2, 3, 64).transpose(0, 2, 1, 3).reshape(72, 384)
-    gains = jnp.stack([gain1, gain2], axis=1)
-    wa = jnp.concatenate([wq, gains, jnp.zeros((72, 62), BF), w_kv], axis=1)
-    wa = jnp.pad(jnp.stack([wa[:, :WA], wa[:, WA:]]), ((0, 0), (0, 8), (0, 0)))
-    wot, wdt = wo.T, wd.T
-    wb = jnp.stack(
-        [
-            jnp.concatenate([wg, wdt[:, :768], wot[:, :512]], axis=1),
-            jnp.concatenate([wu, wdt[:, 768:], wot[:, 512:], jnp.zeros((72, 448), BF)], axis=1),
-        ]
-    )
-    wb = jnp.pad(wb, ((0, 0), (0, 8), (0, 0)))
     cos, sin = tables()
+    cols, rows = placements()
 
     def v(shape, dtype=BF):
         return pltpu.VMEM(shape, dtype)
@@ -630,7 +885,10 @@
     any_space = pl.BlockSpec(memory_space=pl.ANY)
     vmem = pl.BlockSpec(memory_space=pltpu.VMEM)
     scratch = [
-        v((16, 32, DP)), v((2, 8, 80, WA)), v((2, 8, 80, WB)),
+        v((D, ROWS)), v((D, ROWS)), v((72, 576)), v((72, 384)), v((72, 576)), v((72, 1536)),
+        v((72, 1536)), v((72, 1536)), v((D, DP)), v((ROWS, ROWS)),
+        v((16, 32, DP)), v((2, 80, WA)), v((2, TB, 80, 128)),
+        v((16, 32, DP)), v((2, 8, 80, WA)), v((2, 3, 4, 4, 4, 80, 128)),
         v((32, 8, 128), F32), v((32, 8, 128), F32),
         v((16, 3, 256, 128)), v((2048, 128), F32), v((ROWS, ROWS)),
         v((3, 128, 768)), v((3, 768, 128)), v((3, 128, 768)), v((3, 768, 128)),
@@ -639,51 +897,56 @@
         v((ROWS, DP), F32), v((ROWS, DP)), v((ROWS, DP), F32), v((ROWS, DP)), v((DP, ROWS)),
         v((ROWS, DP)), v((ROWS, DP), F32),
         v((4, 4, 3, 256, 128)), v((4, 2, 3, 256, 128)), v((4, 2, 3, 256, 128)),
-        v((8, 3, 256, 128)),
-        v((2, 8, 80, WA)), v((8, 80, WA)), v((8, 80, WB)),
-        v((3, 2, 80, WA)), v((3, 2, 80, WB)), v((2, 80, WA)), v((2, 80, WB)),
-        v((80, WA)), v((80, WB)), v((80, WA)), v((80, WB)),
-        v((80, WA // 2)), v((80, WB // 2)), v((80, WA // 2)), v((80, WB // 2)),
-        v((3, 80, WA // 2)), v((3, 80, WB // 2)), v((2, 80, WA)), v((2, 80, WB)),
+        v((3, 2, 3, 256, 128)), v((3, 256, 128)), v((3, 256, 128)),
+        v((2, 8, 80, WA)), v((8, 80, WA)), v((7, 80, WA)),
+        v((4, 80, 128)), v((8, 80, 128)), v((2, 4, 80, 128)),
+        v((3, 4, 4, 4, 80, 128)), v((3, 3, 4, 4, 80, 128)), v((3, 4, 4, 80, 128)),
+        v((3, 3, 4, 80, 128)), v((3, 4, 80, 128)),
+        v((3, 3, 80, 128)), v((2, 4, 2, 3, 80, 128)),
         v((16, 16, DP)), v((16, 16, DP)), v((16, 16, DP)), v((16, 16, DP)),
-        pltpu.SemaphoreType.DMA((140,)), pltpu.SemaphoreType.DMA((140,)),
-        pltpu.SemaphoreType.DMA((5,)),
+        pltpu.SemaphoreType.DMA((184,)), pltpu.SemaphoreType.DMA((184,)),
+        pltpu.SemaphoreType.DMA((17,)),
     ]
     bo, ig, ga, gb = pl.pallas_call(
         kernel,
         out_shape=(
             jax.ShapeDtypeStruct((16, 16, DP), BF),
             jax.ShapeDtypeStruct((16, 16, DP), BF),
-            jax.ShapeDtypeStruct((2, 80, WA), BF),
-            jax.ShapeDtypeStruct((2, 80, WB), BF),
+            jax.ShapeDtypeStruct((2, 4, 80, 128), BF),
+            jax.ShapeDtypeStruct((2, 4, 2, 3, 80, 128), BF),
         ),
-        in_specs=[any_space] * 5,
+        in_specs=[pl.BlockSpec(memory_space=pltpu.SMEM)] + [vmem] * 2 + [any_space] * 12,
         out_specs=(vmem,) * 4,
         scratch_shapes=scratch,
         compiler_params=pltpu.CompilerParams(
             collective_id=0, has_side_effects=True, vmem_limit_bytes=62 * 1024 * 1024
         ),
         name="layer",
-    )(xc, wa, wb, jnp.asarray(cos), jnp.asarray(sin))
-
-    ga = ga[:, :72].astype(F32)
-    gb = gb[:, :72].astype(F32)
-    g_q = jnp.concatenate([ga[0], ga[1, :, :64]], axis=1)
-    g_kv = ga[1, :, 128:512].reshape(72, 3, 2, 64).transpose(0, 2, 1, 3).reshape(72, 384)
-    g_out = jnp.concatenate([gb[0, :, 2304:2816], gb[1, :, 2304:2368]], axis=1).T
-    g_down = jnp.concatenate([gb[0, :, 1536:2304], gb[1, :, 1536:2304]], axis=1).T
-    return (
-        by_token(bo),
-        by_token(ig).astype(F32),
-        ga[1, :, 64],
-        g_q,
-        g_kv,
-        g_out,
-        ga[1, :, 65],
-        gb[0, :, :1536],
-        gb[1, :, :1536],
-        g_down,
+    )(
+        positions, gain1.reshape(1, 72), gain2.reshape(1, 72), tokens[0].T, cotangent[0].T,
+        wq, wkv, wo.T, wg, wu, wd.T, cols, rows, jnp.asarray(cos), jnp.asarray(sin),
     )
+
+    def f32(*shape):
+        return jax.ShapeDtypeStruct(shape, F32)
+
+    outs = pl.pallas_call(
+        finish,
+        out_shape=(
+            jax.ShapeDtypeStruct((D, ROWS), BF), f32(D, ROWS), f32(1, 72), f32(72, 576),
+            f32(72, 384), f32(72, 576), f32(1, 72), f32(72, 1536), f32(72, 1536), f32(72, 1536),
+        ),
+        in_specs=[any_space] * 6,
+        out_specs=(vmem,) * 10,
+        scratch_shapes=[
+            v((16, 16, DP)), v((16, 16, DP)), v((2, 4, 80, 128)), v((2, 4, 2, 3, 80, 128)),
+            v((D, DP)), v((ROWS, ROWS)), pltpu.SemaphoreType.DMA((6,)),
+        ],
+        compiler_params=pltpu.CompilerParams(vmem_limit_bytes=60 * 1024 * 1024),
+        name="finish",
+    )(bo, ig, ga, gb, cols, rows)
+    out, grad_in, n1, gq, gkv, go, n2, gg, gu, gd = outs
+    return out.T[None], grad_in.T[None], n1.reshape(72), gq, gkv, go.T, n2.reshape(72), gg, gu, gd.T
 
 
 def solution(mesh):

time: 214 us -> 163 us (0.76)
  Pallas kernels: 189 us -> 160 us
  local copies, waits for them, and re-layouts: 13.5 us -> 0 us
  other arithmetic: 6.98 us -> 0 us
    pallas_call x1, Pallas kernels: 189 us -> 156 us  [local(): pl.pallas_call(kernel, out_shape=(jax.ShapeDtypeStruct((16, 16, DP), BF),...]
    pallas_call x0 -> x1, Pallas kernels: none -> 4.42 us  [local(): pl.pallas_call(finish, out_shape=(jax.ShapeDtypeStruct((D, ROWS), BF), f3...]
    unnamed x27 -> x0, local copies, waits for them, and re-layouts: 3.48 us -> none
    slice x5 -> x0, local copies, waits for them, and re-layouts: 3.33 us -> none  [the longest x1 1.01 us: local(): wdt[:, :768]]
where the time goes in v2:
time: 163 us; the launch traced here: 161 us
  Pallas kernels  160 us (98%)
    pallas_call x1, Pallas kernels, local(): pl.pallas_call(kernel, out_shape=(jax.ShapeDtypeStruct((16, 16, DP), BF),...  156 us
    pallas_call x1, Pallas kernels, local(): pl.pallas_call(finish, out_shape=(jax.ShapeDtypeStruct((D, ROWS), BF), f3...  4.42 us

profile of v2, /device:TPU:23, one launch (start us, length us, event | category | flops | bytes accessed | tf_op | source)
XLA Modules:
  0.0 161.2 jit_solution(5850257321248702297)
XLA Ops:
  0.6 156.0 %layer.1 = (bf16[16,16,640]{2,1,0:T(8,128)(2,1)}, bf16[16,16,640]{2,1,0:T(8,128)(2,1)}, bf16[2,4,80,128]{3,2,1,0:T(8,128)(2,1)}, bf16[2,4,2,3,80,128]{5,4,3,2,1,0:T(8,128)(2,1)}) custom-call(s32[1,256]{1,0:T(1,128)} %pos.1, bf16[1,72]{1,0:T(2,128)(2,1)} %bitcast.24, bf16[1,72]{1,0:T(2,128)(2,1)} %bitcast.25, bf16[576,256]{1,0:T(8,128)(2,1)} %bitcast.20, ...), custom_call_target="tpu_custom_call" | custom-call | tf_op jit(solution)/shard_map/layer/pallas_call | solution.py:910
  156.6 4.4 %finish.1 = (bf16[576,256]{1,0:T(8,128)(2,1)}, f32[576,256]{1,0:T(8,128)}, f32[1,72]{1,0:T(1,128)}, f32[72,576]{1,0:T(8,128)}, f32[72,384]{1,0:T(8,128)}, /*inde...) custom-call(bf16[16,16,640]{2,1,0:T(8,128)(2,1)} %get-tuple-element.24.bo_h,, ...), custom_call_target="tpu_custom_call" | custom-call | tf_op jit(solution)/shard_map/finish/pallas_call | solution.py:933

commit v3 on v2

--- a/solution.py
+++ b/solution.py
@@ -209,7 +209,8 @@
 
     sem_x = take(16)
     for step in range(1, 16):
-        send(xc.at[(c + step) % 16], xc_r.at[c], sem_x + step, f, (c + step) % 16)
+        to = (c + step) % 16
+        send(xc.at[to, 0:16], xc_r.at[c, 0:16], sem_x + step, f, to)
     local = [
         pltpu.make_async_copy(xc.at[c], xc_r.at[c], ls.at[0]),
         pltpu.make_async_copy(wa_in.at[k], wa.at[k, f], ls.at[1]),
@@ -276,6 +277,10 @@
     sem_a = take(8)
     gather_first(wa_in, wa, sem_a)
     spread(0)
+    sem_c = take(16)
+    for step in range(1, 16):
+        to = (c + step) % 16
+        send(xc.at[to, 16:32], xc_r.at[c, 16:32], sem_c + step, f, to)
 
     def make_bias(slot, carry):
         e = ctx_at((slot // 2) % 2, slot // 4, slot % 2)
@@ -289,8 +294,9 @@
     gather_second(wa, sem_a)
     for copy in local:
         copy.wait()
+    from_wb = spread(1)
     for step in range(1, 16):
-        arrived(xc_r.at[(c + 16 - step) % 16], sem_x + step)
+        arrived(xc_r.at[(c + 16 - step) % 16, 0:16], sem_x + step)
 
     x_raw = xc_r[:, 0:16, :].reshape(ROWS, DP)
     lane = lane_iota((ROWS, DP))
@@ -301,9 +307,7 @@
     x = mm(perm_t, x_raw)
     x = jnp.where(lane % 80 < 72, x, 0.0)
     xs[...] = x
-    dy[...] = mm(perm_t, xc_r[:, 16:32, :].reshape(ROWS, DP)).astype(BF)
-
-    from_wb = spread(1)
+
     gather_third(wa, sem_a)
     r1 = lax.rsqrt(jnp.sum(x * x, axis=-1, keepdims=True) * (1.0 / D) + 1e-5)
     gather_last(wa, sem_a)
@@ -335,7 +339,7 @@
     near = slot_at(1 - zl, yy, k)
 
     def kv_along_y(slot, a):
-        for off in STEPS[1:]:
+        for off in (1, 3):
             send(kv.at[slot], kv.at[slot], sem_k + a * 4 + off, f, ctx_at(zl, (yy + off) % 4, k))
 
     send(kv.at[mine], kv.at[mine], sem_k, f, other)
@@ -348,6 +352,9 @@
                 at = slot_at(zl if a == 0 else 1 - zl, (yy + 4 - off) % 4, k)
                 arrived(kv.at[at], sem_k + a * 4 + off)
                 send(kv.at[at], kv.at[at], sem_k + 8 + a * 4 + off, f, other)
+                if (a, off) in ((0, 1), (1, 3)):
+                    to = ctx_at(zl, (yy + off) % 4, k)
+                    send(kv.at[at], kv.at[at], sem_k + a * 4 + 2, f, to)
 
     def kv_across(off):
         for a in (0, 1):
@@ -373,6 +380,10 @@
 
     kv_direct(0)
     kv_along_y(near, 1)
+
+    for step in range(1, 16):
+        arrived(xc_r.at[(c + 16 - step) % 16, 16:32], sem_c + step)
+    dy[...] = mm_tn(perm[...], xc_r[:, 16:32, :].reshape(ROWS, DP)).astype(BF)
 
     st_m[...] = jnp.full(st_m.shape, NEG, F32)
     st_l[...] = jnp.zeros(st_l.shape, F32)
@@ -580,43 +591,34 @@
     def red_six():
         arrived(gbf.at[1 - k], sem_r + 38)
 
-    sem_g = take(24)
-
-    def in_core():
-        send(ga.at[1 - k], gac, sem_g, f, other)
-
-    def in_one():
-        arrived(gac, sem_g)
-        ga[k] = (ga[k].astype(F32) + gac[...].astype(F32)).astype(BF)
+    sem_g = take(36)
+
+    def in_core(p):
+        send(ga.at[p, 1 - k], gac.at[p], sem_g + 18 * p, f, other)
+
+    def in_one(p):
+        arrived(gac.at[p], sem_g + 18 * p)
+        ga[p, k] = (ga[p, k].astype(F32) + gac[p].astype(F32)).astype(BF)
         for step in range(1, 8):
             to = (f + step) % 8
-            send(ga.at[k, to], gax.at[step - 1], sem_g + step, to, c)
-
-    def in_two():
+            send(ga.at[p, k, to], gax.at[p, step - 1], sem_g + 18 * p + step, to, c)
+
+    def in_two(p):
         for step in range(1, 8):
-            arrived(gax.at[step - 1], sem_g + step)
-        v = add(ga, (k, f), [gax[i] for i in range(7)])
-        for t in range(4):
-            gay_s[t] = v[:, 128 * t : 128 * t + 128].astype(BF)
+            arrived(gax.at[p, step - 1], sem_g + 18 * p + step)
+        gay_s[p] = add(ga, (p, k, f), [gax[p, i] for i in range(7)]).astype(BF)
         for a, off in CHIPS:
-            y = (yy + off) % 4
-            to = ctx_at(zl if a == 0 else 1 - zl, y, k)
-            send(gay_s.at[y], gay.at[4 * a + off], sem_g + 8 + 4 * a + off, f, to)
-
-    def in_three():
+            to = ctx_at(zl if a == 0 else 1 - zl, (yy + off) % 4, k)
+            send(gay_s.at[p], gay.at[p, 4 * a + off], sem_g + 18 * p + 8 + 4 * a + off, f, to)
+
+    def in_three(p):
         for a, off in CHIPS:
-            arrived(gay.at[4 * a + off], sem_g + 8 + 4 * a + off)
-        gaf[k, yy] = add(gay_s, yy, [gay[4 * a + off] for a, off in CHIPS]).astype(BF)
-        for step in range(1, 4):
-            send(gaf.at[k, yy], gaf.at[k, yy], sem_g + 16 + step, *along(0, "y", step))
-
-    def in_four():
-        for step in range(1, 4):
-            arrived(gaf.at[k, (yy + 4 - step) % 4], sem_g + 16 + step)
-        send(gaf.at[k], gaf.at[k], sem_g + 20, f, other)
-
-    def in_five():
-        arrived(gaf.at[1 - k], sem_g + 20)
+            arrived(gay.at[p, 4 * a + off], sem_g + 18 * p + 8 + 4 * a + off)
+        gaf[p, k] = add(gay_s, p, [gay[p, 4 * a + off] for a, off in CHIPS]).astype(BF)
+        send(gaf.at[p, k], gaf.at[p, k], sem_g + 18 * p + 16, f, other)
+
+    def in_four(p):
+        arrived(gaf.at[p, 1 - k], sem_g + 18 * p + 16)
 
     red_core(0)
     red_core(1)
@@ -727,12 +729,15 @@
     fold_backward(2, BACK[2])
     dkv_first(2)
     dkv_second(2, BACK[2])
-    for n in range(3):
-        red_two(n)
     fold_backward(3, BACK[3])
     dkv_first(3)
-    for n in range(3):
-        red_three(n)
+    for n in (1, 0, 2):
+        red_two(n)
+    dkv_second(3, BACK[3])
+    for off in range(1, 4):
+        arrived(d2_r.at[off - 1], sem_d + off)
+    dz_s[...] = add(d2_s, (3, 1 - zl), [d2_r[i, 1 - zl] for i in range(3)]).astype(BF)
+    send(dz_s, dz_r, sem_d, f, ctx_at(1 - zl, yy, k))
 
     dq_tiles = []
     for t in range(5):
@@ -745,16 +750,16 @@
         dq_tiles.append((u * cos - partner_lanes(u) * sin).astype(BF))
     dq = jnp.concatenate(dq_tiles, axis=1)
     a1t = act1t[...]
-    ga[0] = mm(a1t, dq[:, 0:512]).astype(BF).reshape(8, 80, 512)
+    grad_q = mm(a1t, dq)
+    for half in range(2):
+        ga[0, half] = grad_q[:, 256 * half : 256 * half + 256].astype(BF).reshape(8, 80, 256)
+    in_core(0)
     dact1 = mm_nt(dq[:, 0:512], wa[0].reshape(DP, 512)) + mm_nt(
         dq[:, 512:640], wa[1, :, :, 0:128].reshape(DP, 128)
     )
-    dkv_second(3, BACK[3])
-    for off in range(1, 4):
-        arrived(d2_r.at[off - 1], sem_d + off)
-    dz_s[...] = add(d2_s, (3, 1 - zl), [d2_r[i, 1 - zl] for i in range(3)]).astype(BF)
-    send(dz_s, dz_r, sem_d, f, ctx_at(1 - zl, yy, k))
-    red_four()
+    in_one(0)
+    for n in (1, 0, 2):
+        red_three(n)
     dkv = add(d2_s, (3, zl), [d2_r[i, zl] for i in range(3)])
     arrived(dz_r, sem_d)
     dkv = dkv + dz_r[...].astype(F32)
@@ -762,7 +767,9 @@
         u = dkv[g]
         u = (u * cos_kv - partner_lanes(u) * sin_kv).astype(BF)
         at = 128 + 128 * g
-        ga[1, :, :, at : at + 128] = mm(a1t, u).astype(BF).reshape(8, 80, 128)
+        part = mm(a1t, u).astype(BF).reshape(8, 80, 128)
+        lanes = slice(128, 256) if g != 1 else slice(0, 128)
+        ga[1, 0 if g == 0 else 1, :, :, lanes] = part
         dact1 = dact1 + mm_nt(u, wa[1, :, :, at : at + 128].reshape(DP, 128))
 
     x = xs[...]
@@ -773,28 +780,31 @@
     )
     hot = jnp.where(lax.broadcasted_iota(jnp.int32, (8, 128), 0) < 2, hot, 0.0)
     gain_cols = mm(gains.T.astype(BF), hot.astype(BF))
-    ga[1, :, :, 0:128] = (mm(a1t, dq[:, 512:640]) + gain_cols).astype(BF).reshape(8, 80, 128)
-    in_core()
+    ga[1, 0, :, :, 0:128] = (grad_q[:, 512:640] + gain_cols).astype(BF).reshape(8, 80, 128)
+    in_core(1)
+    red_four()
 
     wgt = dact1 * gain1
     inner = jnp.sum(wgt * x, axis=-1, keepdims=True) * (1.0 / D)
     give_back(
         dmid[...] + r1 * wgt - x * (r1 * r1 * r1) * inner, ig_s, ig_r, sem_i
     )
-    in_one()
+    in_one(1)
+    in_two(0)
+    in_two(1)
     red_five()
+    in_three(0)
     for step in range(1, 16):
         arrived(bo_r.at[(c + 16 - step) % 16], sem_o + step)
     bo_out[...] = bo_r[...]
-    red_six()
-    gb_out[...] = gbf[...]
-    in_two()
-    in_three()
+    in_three(1)
     for step in range(1, 16):
         arrived(ig_r.at[(c + 16 - step) % 16], sem_i + step)
     ig_out[...] = ig_r[...]
-    in_four()
-    in_five()
+    red_six()
+    gb_out[...] = gbf[...]
+    in_four(0)
+    in_four(1)
     ga_out[...] = gaf[...]
     for copy in sends:
         copy.wait_send()
@@ -843,16 +853,16 @@
         return ref[at].astype(F32)
 
     for t in range(4):
-        gq[:, 128 * t : 128 * t + 128] = part(ga, 0, t)[0:72]
-    last = part(ga, 1, 0)
+        gq[:, 128 * t : 128 * t + 128] = part(ga, 0, t // 2)[0:72, 128 * (t % 2) : 128 * (t % 2) + 128]
+    last = part(ga, 1, 0)[:, 0:128]
     gq[:, 512:576] = last[0:72, 0:64]
     row = lax.broadcasted_iota(jnp.int32, (16, 128), 0)
     hot = jnp.where((lane_iota((16, 128)) == 64 + row) & (row < 2), 1.0, 0.0).astype(BF)
-    gains = mm_nt(hot, ga[1, 0])
+    gains = mm_nt(hot, last.astype(BF))
     n1[...] = gains[0:1, 0:72]
     n2[...] = gains[1:2, 0:72]
     low = lane_iota((80, 128)) < 64
-    tiles = [part(ga, 1, 1 + g) for g in range(3)]
+    tiles = [part(ga, 1, 0)[:, 128:256], part(ga, 1, 1)[:, 0:128], part(ga, 1, 1)[:, 128:256]]
     turn = [pltpu.roll(t, 64, 1) for t in tiles]
     heads = [
         jnp.where(low, tiles[0], turn[1]),
@@ -898,13 +908,13 @@
         v((ROWS, DP)), v((ROWS, DP), F32),
         v((4, 4, 3, 256, 128)), v((4, 2, 3, 256, 128)), v((4, 2, 3, 256, 128)),
         v((3, 2, 3, 256, 128)), v((3, 256, 128)), v((3, 256, 128)),
-        v((2, 8, 80, WA)), v((8, 80, WA)), v((7, 80, WA)),
-        v((4, 80, 128)), v((8, 80, 128)), v((2, 4, 80, 128)),
+        v((2, 2, 8, 80, 256)), v((2, 8, 80, 256)), v((2, 7, 80, 256)),
+        v((2, 80, 256)), v((2, 8, 80, 256)), v((2, 2, 80, 256)),
         v((3, 4, 4, 4, 80, 128)), v((3, 3, 4, 4, 80, 128)), v((3, 4, 4, 80, 128)),
         v((3, 3, 4, 80, 128)), v((3, 4, 80, 128)),
         v((3, 3, 80, 128)), v((2, 4, 2, 3, 80, 128)),
         v((16, 16, DP)), v((16, 16, DP)), v((16, 16, DP)), v((16, 16, DP)),
-        pltpu.SemaphoreType.DMA((184,)), pltpu.SemaphoreType.DMA((184,)),
+        pltpu.SemaphoreType.DMA((216,)), pltpu.SemaphoreType.DMA((216,)),
         pltpu.SemaphoreType.DMA((17,)),
     ]
     bo, ig, ga, gb = pl.pallas_call(
@@ -912,7 +922,7 @@
         out_shape=(
             jax.ShapeDtypeStruct((16, 16, DP), BF),
             jax.ShapeDtypeStruct((16, 16, DP), BF),
-            jax.ShapeDtypeStruct((2, 4, 80, 128), BF),
+            jax.ShapeDtypeStruct((2, 2, 80, 256), BF),
             jax.ShapeDtypeStruct((2, 4, 2, 3, 80, 128), BF),
         ),
         in_specs=[pl.BlockSpec(memory_space=pltpu.SMEM)] + [vmem] * 2 + [any_space] * 12,
@@ -939,7 +949,7 @@
         in_specs=[any_space] * 6,
         out_specs=(vmem,) * 10,
         scratch_shapes=[
-            v((16, 16, DP)), v((16, 16, DP)), v((2, 4, 80, 128)), v((2, 4, 2, 3, 80, 128)),
+            v((16, 16, DP)), v((16, 16, DP)), v((2, 2, 80, 256)), v((2, 4, 2, 3, 80, 128)),
             v((D, DP)), v((ROWS, ROWS)), pltpu.SemaphoreType.DMA((6,)),
         ],
         compiler_params=pltpu.CompilerParams(vmem_limit_bytes=60 * 1024 * 1024),

time: 163 us -> 153 us (0.939)
  Pallas kernels: 160 us -> 151 us
    pallas_call x1, Pallas kernels: 156 us -> 146 us  [local(): pl.pallas_call(kernel, out_shape=(jax.ShapeDtypeStruct((16, 16, DP), BF),...]
where the time goes in v3:
time: 153 us; the launch traced here: 151 us
  Pallas kernels  151 us (99%)
    pallas_call x1, Pallas kernels, local(): pl.pallas_call(kernel, out_shape=(jax.ShapeDtypeStruct((16, 16, DP), BF),...  146 us
    pallas_call x1, Pallas kernels, local(): pl.pallas_call(finish, out_shape=(jax.ShapeDtypeStruct((D, ROWS), BF), f3...  4.42 us

profile of v3, /device:TPU:23, one launch (start us, length us, event | category | flops | bytes accessed | tf_op | source)
XLA Modules:
  0.0 151.5 jit_solution(12794932889889330978)
XLA Ops:
  0.6 146.2 %layer.1 = (bf16[16,16,640]{2,1,0:T(8,128)(2,1)}, bf16[16,16,640]{2,1,0:T(8,128)(2,1)}, bf16[2,2,80,256]{3,2,1,0:T(8,128)(2,1)}, bf16[2,4,2,3,80,128]{5,4,3,2,1,0:T(8,128)(2,1)}) custom-call(s32[1,256]{1,0:T(1,128)} %pos.1, bf16[1,72]{1,0:T(2,128)(2,1)} %bitcast.24, bf16[1,72]{1,0:T(2,128)(2,1)} %bitcast.25, bf16[576,256]{1,0:T(8,128)(2,1)} %bitcast.20, ...), custom_call_target="tpu_custom_call" | custom-call | tf_op jit(solution)/shard_map/layer/pallas_call | solution.py:920
  146.9 4.4 %finish.1 = (bf16[576,256]{1,0:T(8,128)(2,1)}, f32[576,256]{1,0:T(8,128)}, f32[1,72]{1,0:T(1,128)}, f32[72,576]{1,0:T(8,128)}, f32[72,384]{1,0:T(8,128)}, /*inde...) custom-call(bf16[16,16,640]{2,1,0:T(8,128)(2,1)} %get-tuple-element.24.bo_h,, ...), custom_call_target="tpu_custom_call" | custom-call | tf_op jit(solution)/shard_map/finish/pallas_call | solution.py:943

commit v4 on v3

--- a/solution.py
+++ b/solution.py
@@ -207,10 +207,6 @@
                 at.append((coord(n, name) + 4 - step) % 4 if name == axis else coord(n, name))
         return wb.at[(k, n, *at)]
 
-    sem_x = take(16)
-    for step in range(1, 16):
-        to = (c + step) % 16
-        send(xc.at[to, 0:16], xc_r.at[c, 0:16], sem_x + step, f, to)
     local = [
         pltpu.make_async_copy(xc.at[c], xc_r.at[c], ls.at[0]),
         pltpu.make_async_copy(wa_in.at[k], wa.at[k, f], ls.at[1]),
@@ -276,6 +272,11 @@
 
     sem_a = take(8)
     gather_first(wa_in, wa, sem_a)
+    sem_x = take(16)
+    for step in range(1, 16):
+        to = (c + step) % 16
+        send(xc.at[to, 0:16], xc_r.at[c, 0:16], sem_x + step, f, to)
+    gather_second(wa, sem_a)
     spread(0)
     sem_c = take(16)
     for step in range(1, 16):
@@ -291,7 +292,6 @@
         return carry
 
     lax.fori_loop(0, 16, make_bias, 0)
-    gather_second(wa, sem_a)
     for copy in local:
         copy.wait()
     from_wb = spread(1)
@@ -362,7 +362,6 @@
             arrived(kv.at[at], sem_k if (a, off) == (0, 0) else sem_k + 8 + a * 4 + off)
 
     from_wb += spread(2)
-
     for t in range(5):
         w = wa[0, :, :, 128 * t : 128 * t + 128] if t < 4 else wa[1, :, :, 0:128]
         u = mm(a1b, w.reshape(DP, 128))
@@ -758,8 +757,6 @@
         dq[:, 512:640], wa[1, :, :, 0:128].reshape(DP, 128)
     )
     in_one(0)
-    for n in (1, 0, 2):
-        red_three(n)
     dkv = add(d2_s, (3, zl), [d2_r[i, zl] for i in range(3)])
     arrived(dz_r, sem_d)
     dkv = dkv + dz_r[...].astype(F32)
@@ -782,14 +779,16 @@
     gain_cols = mm(gains.T.astype(BF), hot.astype(BF))
     ga[1, 0, :, :, 0:128] = (grad_q[:, 512:640] + gain_cols).astype(BF).reshape(8, 80, 128)
     in_core(1)
-    red_four()
+    in_one(1)
+    for n in (1, 0, 2):
+        red_three(n)
 
     wgt = dact1 * gain1
     inner = jnp.sum(wgt * x, axis=-1, keepdims=True) * (1.0 / D)
     give_back(
         dmid[...] + r1 * wgt - x * (r1 * r1 * r1) * inner, ig_s, ig_r, sem_i
     )
-    in_one(1)
+    red_four()
     in_two(0)
     in_two(1)
     red_five()

time: 153 us -> 153 us (level)
  no operation moved by 1% of the time
where the time goes in v4:
time: 153 us
  Pallas kernels  152 us (99%)
    pallas_call x1, Pallas kernels, local(): pl.pallas_call(kernel, out_shape=(jax.ShapeDtypeStruct((16, 16, DP), BF),...  147 us
    pallas_call x1, Pallas kernels, local(): pl.pallas_call(finish, out_shape=(jax.ShapeDtypeStruct((D, ROWS), BF), f3...  4.42 us

profile of v4, /device:TPU:23, one launch (start us, length us, event | category | flops | bytes accessed | tf_op | source)
XLA Modules:
  0.0 152.7 jit_solution(4588223914168472086)
XLA Ops:
  0.6 147.4 %layer.1 = (bf16[16,16,640]{2,1,0:T(8,128)(2,1)}, bf16[16,16,640]{2,1,0:T(8,128)(2,1)}, bf16[2,2,80,256]{3,2,1,0:T(8,128)(2,1)}, bf16[2,4,2,3,80,128]{5,4,3,2,1,0:T(8,128)(2,1)}) custom-call(s32[1,256]{1,0:T(1,128)} %pos.1, bf16[1,72]{1,0:T(2,128)(2,1)} %bitcast.24, bf16[1,72]{1,0:T(2,128)(2,1)} %bitcast.25, bf16[576,256]{1,0:T(8,128)(2,1)} %bitcast.20, ...), custom_call_target="tpu_custom_call" | custom-call | tf_op jit(solution)/shard_map/layer/pallas_call | solution.py:919
  148.1 4.4 %finish.1 = (bf16[576,256]{1,0:T(8,128)(2,1)}, f32[576,256]{1,0:T(8,128)}, f32[1,72]{1,0:T(1,128)}, f32[72,576]{1,0:T(8,128)}, f32[72,384]{1,0:T(8,128)}, /*inde...) custom-call(bf16[16,16,640]{2,1,0:T(8,128)(2,1)} %get-tuple-element.24.bo_h,, ...), custom_call_target="tpu_custom_call" | custom-call | tf_op jit(solution)/shard_map/finish/pallas_call | solution.py:942

commit v5 on v4

--- a/solution.py
+++ b/solution.py
@@ -96,6 +96,11 @@
         copy.start()
         sends.append(copy)
         return copy
+
+    def drain(count):
+        for copy in sends[:count]:
+            copy.wait_send()
+        del sends[:count]
 
     def arrived(dst, sem):
         remote(dst, dst, sem, f, other).wait_recv()
@@ -736,6 +741,7 @@
     for off in range(1, 4):
         arrived(d2_r.at[off - 1], sem_d + off)
     dz_s[...] = add(d2_s, (3, 1 - zl), [d2_r[i, 1 - zl] for i in range(3)]).astype(BF)
+    old = len(sends)
     send(dz_s, dz_r, sem_d, f, ctx_at(1 - zl, yy, k))
 
     dq_tiles = []
@@ -757,6 +763,7 @@
         dq[:, 512:640], wa[1, :, :, 0:128].reshape(DP, 128)
     )
     in_one(0)
+    drain(old)
     dkv = add(d2_s, (3, zl), [d2_r[i, zl] for i in range(3)])
     arrived(dz_r, sem_d)
     dkv = dkv + dz_r[...].astype(F32)
@@ -778,6 +785,7 @@
     hot = jnp.where(lax.broadcasted_iota(jnp.int32, (8, 128), 0) < 2, hot, 0.0)
     gain_cols = mm(gains.T.astype(BF), hot.astype(BF))
     ga[1, 0, :, :, 0:128] = (grad_q[:, 512:640] + gain_cols).astype(BF).reshape(8, 80, 128)
+    old = len(sends)
     in_core(1)
     in_one(1)
     for n in (1, 0, 2):
@@ -790,9 +798,12 @@
     )
     red_four()
     in_two(0)
+    drain(old)
+    old = len(sends)
     in_two(1)
     red_five()
     in_three(0)
+    drain(old)
     for step in range(1, 16):
         arrived(bo_r.at[(c + 16 - step) % 16], sem_o + step)
     bo_out[...] = bo_r[...]

time: 153 us -> 153 us (level)
  no operation moved by 1% of the time
where the time goes in v5:
time: 153 us; the launch traced here: 152 us
  Pallas kernels  152 us (99%)
    pallas_call x1, Pallas kernels, local(): pl.pallas_call(kernel, out_shape=(jax.ShapeDtypeStruct((16, 16, DP), BF),...  147 us
    pallas_call x1, Pallas kernels, local(): pl.pallas_call(finish, out_shape=(jax.ShapeDtypeStruct((D, ROWS), BF), f3...  4.42 us

profile of v5, /device:TPU:23, one launch (start us, length us, event | category | flops | bytes accessed | tf_op | source)
XLA Modules:
  0.0 152.4 jit_solution(15591039057828278051)
XLA Ops:
  0.6 147.2 %layer.1 = (bf16[16,16,640]{2,1,0:T(8,128)(2,1)}, bf16[16,16,640]{2,1,0:T(8,128)(2,1)}, bf16[2,2,80,256]{3,2,1,0:T(8,128)(2,1)}, bf16[2,4,2,3,80,128]{5,4,3,2,1,0:T(8,128)(2,1)}) custom-call(s32[1,256]{1,0:T(1,128)} %pos.1, bf16[1,72]{1,0:T(2,128)(2,1)} %bitcast.24, bf16[1,72]{1,0:T(2,128)(2,1)} %bitcast.25, bf16[576,256]{1,0:T(8,128)(2,1)} %bitcast.20, ...), custom_call_target="tpu_custom_call" | custom-call | tf_op jit(solution)/shard_map/layer/pallas_call | solution.py:930
  147.8 4.4 %finish.1 = (bf16[576,256]{1,0:T(8,128)(2,1)}, f32[576,256]{1,0:T(8,128)}, f32[1,72]{1,0:T(1,128)}, f32[72,576]{1,0:T(8,128)}, f32[72,384]{1,0:T(8,128)}, /*inde...) custom-call(bf16[16,16,640]{2,1,0:T(8,128)(2,1)} %get-tuple-element.24.bo_h,, ...), custom_call_target="tpu_custom_call" | custom-call | tf_op jit(solution)/shard_map/finish/pallas_call | solution.py:953
